TPU v7x, 32 devices: a whole 2x2x4 slice. The times are simulated.
32 devices in a mesh: groups: 2 (over x), dp: 4 (over y, core), tensor: 4 (over z).
Axes of the slice: x: 2, y: 2, z: 4, core: 2. Of those that a mesh axis runs over, the one named last changes fastest.
Arguments:
- tokens: bfloat16 [16, 256, 4096], P(('groups', 'dp'), None, 'tensor'), parts along dimension 0, may hold values from -6 to 6
- ln_gain: float32 [4096], replicated, may hold values from 0.5 to 1.5
- w_query: bfloat16 [4096, 2048], P(None, 'tensor'), may hold values from -0.375 to 0.375
- w_key: bfloat16 [4096, 2048], P(None, 'tensor'), may hold values from -0.09375 to 0.09375
- w_value: bfloat16 [4096, 2048], P(None, 'tensor'), may hold values from -0.09375 to 0.09375
- w_out: bfloat16 [2048, 4096], P('tensor'), may hold values from -0.125 to 0.125
- final_gain: float32 [4096], replicated, may hold values from 0.5 to 1.5
- w_cross_key: bfloat16 [4096, 2048], P(None, 'tensor'), may hold values from -0.09375 to 0.09375
- w_cross_value: bfloat16 [4096, 2048], P(None, 'tensor'), may hold values from -0.09375 to 0.09375
- dec_query: bfloat16 [8, 32, 2048], P(('groups', 'dp'), None, 'tensor'), parts along dimension 0, may hold values from -24 to 24
- grad_out: bfloat16 [8, 32, 2048], P(('groups', 'dp'), None, 'tensor'), parts along dimension 0, may hold values from -6 to 6
- passage_query: int32 [16, 1], P('groups'), parts along dimension 0, may hold values from 0 to 3
- passage_length: int32 [16], P('groups'), parts along dimension 0, may hold values from 1 to 256, 1536 in all
Outputs:
- attended: bfloat16 [8, 32, 2048], P(('groups', 'dp'), None, 'tensor'), parts along dimension 0
- d_query: bfloat16 [8, 32, 2048], P(('groups', 'dp'), None, 'tensor'), parts along dimension 0
- d_values: bfloat16 [16, 256, 2048], P(('groups', 'dp'), None, 'tensor'), parts along dimension 0
There are 2 independent parts, one for each index of `groups`. A program takes and returns all parts, laid end to end along the dimension named above; an argument that names none is the same for every part. Nothing has to cross between parts.
Inputs may be any that keep to these rules, and one draw needn't show every extreme that they name: `passage_query`: every query owns at least one passage.
All inputs are finite; a program needn't handle non-finite values.
Results may differ from a plain program's by a relative error of at most 0.04.
Values may be sent and summed in bfloat16 or wider, within the bound.
A program may use at most 128 MiB of HBM per device.

v0:
```python
import jax
import jax.numpy as jnp
from jax import lax
from jax.sharding import PartitionSpec as P

HD = 64


blocked = -1e30


def norm_rows(values, gain):
    return values * lax.rsqrt(jnp.mean(values * values, axis=-1, keepdims=True) + 1e-06) * gain


def backward_terms(probs, low, out_grad, row_delta, key_heads, value_heads):
    grad_probs = jnp.einsum(
        "aihd,thd->ahit", out_grad, value_heads, preferred_element_type=jnp.float32
    )
    grad_scores = (
        probs * (grad_probs - jnp.transpose(row_delta, (0, 2, 1))[:, :, :, None])
    ).astype(jnp.bfloat16)
    query_term = jnp.einsum(
        "ahit,thd->aihd", grad_scores, key_heads, preferred_element_type=jnp.float32
    )
    value_term = jnp.einsum("ahit,aihd->thd", low, out_grad, preferred_element_type=jnp.float32)
    return (query_term, value_term)


def shards(
    tokens,
    ln_gain,
    w_query,
    w_key,
    w_value,
    w_out,
    final_gain,
    w_cross_key,
    w_cross_value,
    dec_query,
    grad_out,
    passage_query,
    passage_length,
):
    pass_dev, seq_len, part_width = tokens.shape
    local_cols = w_query.shape[1]
    local_heads = local_cols // HD
    score_scale = HD ** (-0.5)
    row_count = pass_dev * seq_len
    query_count = dec_query.shape[0]
    dec_len = dec_query.shape[1]
    gathered_in = lax.all_gather(tokens, "tensor", axis=2, tiled=True)
    full_width = gathered_in.shape[2]
    inputs_f = gathered_in.reshape(row_count, full_width).astype(jnp.float32)
    normed = norm_rows(inputs_f, ln_gain).astype(jnp.bfloat16)

    def project(weight):
        return (
            jnp.dot(normed, weight, preferred_element_type=jnp.float32)
            .astype(jnp.bfloat16)
            .reshape(pass_dev, seq_len, local_heads, HD)
        )

    self_queries = project(w_query)
    self_keys = project(w_key)
    self_values = project(w_value)
    pass_start = lax.axis_index("dp") * pass_dev
    own_length = lax.dynamic_slice_in_dim(passage_length, pass_start, pass_dev)
    positions = jnp.arange(seq_len, dtype=jnp.int32)
    own_valid = positions[None, :] < own_length[:, None]
    scores = (
        jnp.einsum("pqhd,pkhd->phqk", self_queries, self_keys, preferred_element_type=jnp.float32)
        * score_scale
    )
    scores = jnp.where(own_valid[:, None, None, :], scores, blocked)
    row_peak = jnp.max(scores, axis=-1, keepdims=True)
    expd = jnp.where(own_valid[:, None, None, :], jnp.exp(scores - row_peak), 0.0)
    weights = (expd / jnp.sum(expd, axis=-1, keepdims=True)).astype(jnp.bfloat16)
    context = (
        jnp.einsum("phqk,pkhd->pqhd", weights, self_values, preferred_element_type=jnp.float32)
        .astype(jnp.bfloat16)
        .reshape(row_count, local_cols)
    )
    partial_value = jnp.dot(context, w_out, preferred_element_type=jnp.float32)
    summed = lax.psum(partial_value.astype(jnp.bfloat16), "tensor").astype(jnp.float32)
    encoded = norm_rows(inputs_f + summed, final_gain).astype(jnp.bfloat16)
    cross_keys = jnp.dot(encoded, w_cross_key, preferred_element_type=jnp.float32).astype(
        jnp.bfloat16
    )
    cross_values = jnp.dot(encoded, w_cross_value, preferred_element_type=jnp.float32).astype(
        jnp.bfloat16
    )
    all_keys, all_values = (
        lax.all_gather(cross_keys, "dp", axis=0, tiled=True),
        lax.all_gather(cross_values, "dp", axis=0, tiled=True),
    )
    token_total = all_keys.shape[0]
    key_heads = all_keys.reshape(token_total, local_heads, HD)
    value_heads = all_values.reshape(token_total, local_heads, HD)
    all_valid = (positions[None, :] < passage_length[:, None]).reshape(-1)
    all_query = jnp.repeat(passage_query[:, 0], seq_len)
    query_ids = lax.axis_index("dp") * query_count + jnp.arange(query_count, dtype=jnp.int32)
    key_mask = ((all_query[None, :] == query_ids[:, None]) & all_valid[None, :])[:, None, None, :]
    query_heads = dec_query.reshape(query_count, dec_len, local_heads, HD)
    out_grad = grad_out.reshape(query_count, dec_len, local_heads, HD)
    cross_scores = (
        jnp.einsum("aihd,thd->ahit", query_heads, key_heads, preferred_element_type=jnp.float32)
        * score_scale
    )
    cross_scores = jnp.where(key_mask, cross_scores, blocked)
    cross_peak = jnp.max(cross_scores, axis=-1, keepdims=True)
    cross_exp = jnp.where(key_mask, jnp.exp(cross_scores - cross_peak), 0.0)
    probs = cross_exp / jnp.sum(cross_exp, axis=-1, keepdims=True)
    low = probs.astype(jnp.bfloat16)
    attended_heads = jnp.einsum(
        "ahit,thd->aihd", low, value_heads, preferred_element_type=jnp.float32
    ).astype(jnp.bfloat16)
    row_delta = jnp.sum(out_grad.astype(jnp.float32) * attended_heads.astype(jnp.float32), axis=-1)
    query_term, value_term = backward_terms(probs, low, out_grad, row_delta, key_heads, value_heads)
    attended = attended_heads.reshape(query_count, dec_len, local_cols)
    d_query = (
        (query_term * score_scale).astype(jnp.bfloat16).reshape(query_count, dec_len, local_cols)
    )
    value_back = lax.psum_scatter(
        value_term.reshape(token_total, local_cols).astype(jnp.bfloat16),
        "dp",
        scatter_dimension=0,
        tiled=True,
    )
    d_values = value_back.reshape(pass_dev, seq_len, local_cols)
    return (attended, d_query, d_values)


def solution(mesh):
    in_specs = (
        P(("groups", "dp"), None, "tensor"),
        P(),
        P(None, "tensor"),
        P(None, "tensor"),
        P(None, "tensor"),
        P("tensor", None),
        P(),
        P(None, "tensor"),
        P(None, "tensor"),
        P(("groups", "dp"), None, "tensor"),
        P(("groups", "dp"), None, "tensor"),
        P("groups", None),
        P("groups"),
    )
    out_specs = (
        P(("groups", "dp"), None, "tensor"),
        P(("groups", "dp"), None, "tensor"),
        P(("groups", "dp"), None, "tensor"),
    )
    return jax.shard_map(shards, mesh=mesh, in_specs=in_specs, out_specs=out_specs, check_vma=False)
```

profile of v0, /device:TPU:0, one launch (start us, length us, event | category | flops | bytes accessed | tf_op | source)
XLA Modules:
  0.0 379.7 jit_solution(1149459254345767881)
XLA Ops:
  7.2 0.7 all-gather.4.cloned.1.call-update
  8.0 0.7 dynamic_slice.3
  8.7 0.1 iota_compare_fusion.1
  8.8 84.3 %all-gather.4.cloned.1.call-done = bf16[2,256,4096]{2,1,0:T(8,128)(2,1)} async-done(((bf16[2,256,1024]{2,1,0:T(8,128)(2,1)}), bf16[2,256,4096]{2,1,0:T(8,128)(2,1)}) %all-gather.4.cloned.1.call-update) | async-done | bytes 4194320 | tf_op jit(solution)/shard_map/all_gather | solution.py:52
  93.1 3.2 fusion.1
  96.3 0.2 copy-done
  96.5 1.7 fusion.3
  98.2 2.0 copy-done.4
  100.2 2.4 convolution_convert_fusion.4
  102.5 0.5 reshape.194
  103.1 6.7 %convolution_convert_fusion.5 = bf16[512,512]{1,0:T(8,128)(2,1)} fusion(bf16[512,4096]{1,0:T(8,128)(2,1)} %copy-done.4, bf16[4096,512]{1,0:T(8,128)(2,1)} %param.15), kind=kOutput, calls=%fused_computation.35 | convolution fusion | flops 2147745792 | bytes 8912896 | tf_op jit(solution)/shard_map/dot_general | solution.py:59
  109.8 2.3 convolution_convert_fusion.6
  112.2 0.5 reshape.192
  112.7 1.8 reshape.193
  114.5 0.7 fusion.26
  115.2 1.7 fusion.43
  117.0 0.5 fusion.20
  117.5 0.5 copy.35
  118.1 0.1 copy.53
  118.2 1.0 copy-done.6
  119.2 4.3 %convolution_convert_fusion = bf16[512,4096]{1,0:T(8,128)(2,1)} fusion(bf16[512,512]{0,1:T(8,128)(2,1)S(1)} %bitcast.107, bf16[512,4096]{1,0:T(8,128)(2,1)S(1)} %copy-done.6), kind=kOutput, calls=%fused_computation.9 | convolution fusion | flops 2149580800 | bytes 8912896 | tf_op jit(solution)/shard_map/dot_general | solution.py:84
  123.5 0.0 all-gather.8.cloned.1.call-start
  123.6 153.6 %all-reduce.2.cloned.1.call-done = bf16[512,4096]{1,0:T(8,128)(2,1)} async-done(((bf16[512,4096]{1,0:T(8,128)(2,1)}), bf16[512,4096]{1,0:T(8,128)(2,1)}) %all-reduce.2.cloned.1.call-update) | async-done | bytes 4194320 | tf_op jit(solution)/shard_map/psum | solution.py:85
  277.2 5.0 %multiply_reduce_fusion = f32[512]{0:T(512)S(1)} fusion(bf16[512,4096]{1,0:T(8,128)(2,1)} %all-reduce.2.cloned.1.call-done, bf16[2,256,4096]{2,1,0:T(8,128)(2,1)} %all-gather.4.cloned.1.call-done), kind=kLoop, calls=%fused_computation.8 | loop fusion | flops 10485248 | bytes 8390656 | tf_op jit(solution)/shard_map/reduce_sum | solution.py:13
  282.3 0.9 copy-done.2
  283.1 2.4 multiply_convert_fusion
  285.6 1.9 copy-done.7
  287.5 3.2 convolution_convert_fusion.2
  290.7 0.0 all-gather.6.cloned.1.call-start
  290.8 6.6 %convolution_convert_fusion.3 = bf16[512,512]{1,0:T(8,128)(2,1)} fusion(bf16[512,4096]{1,0:T(8,128)(2,1)} %copy-done.7, bf16[4096,512]{1,0:T(8,128)(2,1)} %param.21), kind=kOutput, calls=%fused_computation.33 | convolution fusion | flops 2147745792 | bytes 8912896 | tf_op jit(solution)/shard_map/dot_general | solution.py:90
  297.4 0.3 reduce-scatter.2.cloned.1.call-start
  297.7 0.1 fusion.37
  297.8 0.1 reshape.186
  297.9 0.1 reshape.183
  298.0 14.4 %all-gather.8.cloned.1.call-done = bf16[2048,512]{1,0:T(8,128)(2,1)} async-done(((bf16[512,512]{1,0:T(8,128)(2,1)}), bf16[2048,512]{1,0:T(8,128)(2,1)}) %all-gather.8.cloned.1.call-update) | async-done | bytes 2097168 | tf_op jit(solution)/shard_map/all_gather | solution.py:94
  312.4 2.9 copy.37
  315.4 0.6 fusion.44
  316.0 0.5 fusion.18
  316.5 2.1 convolution_convert_fusion.1
  318.6 0.1 reshape.191
  318.7 18.5 %all-gather.6.cloned.1.call-done = bf16[2048,512]{1,0:T(8,128)(2,1)} async-done(((bf16[512,512]{1,0:T(8,128)(2,1)}), bf16[2048,512]{1,0:T(8,128)(2,1)}) %all-gather.6.cloned.1.call-update) | async-done | bytes 2097168 | tf_op jit(solution)/shard_map/all_gather | solution.py:95
  337.1 4.0 %copy.36 = bf16[2048,512]{0,1:T(8,128)(2,1)} copy(bf16[2048,512]{1,0:T(8,128)(2,1)} %all-gather.6.cloned.1.call-done) | data formatting | bytes 4194304 | tf_op jit(solution)/shard_map/all_gather | solution.py:95
  341.1 3.0 fusion.32
  344.1 3.8 fusion.22
  347.9 0.7 reshape.188
  348.7 0.7 reshape.185
  349.4 21.7 %reduce-scatter.2.cloned.1.call-done = bf16[512,512]{0,1:T(8,128)(2,1)} async-done(((bf16[2048,512]{0,1:T(8,128)(2,1)}), bf16[512,512]{0,1:T(8,128)(2,1)}) %reduce-scatter.2.cloned.1.call-update) | async-done | bytes 524304 | tf_op jit(solution)/shard_map/reduce_scatter | solution.py:124
  371.2 2.0 copy.44
  (42 shorter events, 0.3 us)
Async XLA Ops:
  7.2 89.2 %copy-start.10 = (f32[4096]{0:T(1024)S(1)}, f32[4096]{0:T(1024)}, u32[]{:S(2)}) copy-start(f32[4096]{0:T(1024)} %param.14) | copy-start | bytes 49156
  7.2 85.9 %all-gather.4.cloned.1.call-start = ((), (), s32[]{:S(2)}) async-start(), calls=%async_computation.1 | async-start | bytes 5242880 | tf_op jit(solution)/shard_map/all_gather | solution.py:52
  7.9 269.3 %all-reduce.2.cloned.1.call-start = ((), (), s32[]{:S(2)}) async-start(), calls=%async_computation.2 | async-start | bytes 8388608 | tf_op jit(solution)/shard_map/psum | solution.py:85
  93.1 3.4 copy-start
  96.5 3.6 copy-start.13
  98.2 2.0 copy-start.4
  103.1 6.7 %copy-start.5 = (bf16[512,4096]{1,0:T(8,128)(2,1)S(1)}, bf16[512,4096]{1,0:T(8,128)(2,1)}, u32[]{:S(2)}) copy-start(bf16[512,4096]{1,0:T(8,128)(2,1)} %copy-done.4) | copy-start | bytes 12582916
  103.1 6.7 %copy-start.14 = (bf16[4096,512]{1,0:T(8,128)(2,1)S(1)}, bf16[4096,512]{1,0:T(8,128)(2,1)}, u32[]{:S(2)}) copy-start(bf16[4096,512]{1,0:T(8,128)(2,1)} %param.17) | copy-start | bytes 12582916
  117.0 2.2 copy-start.6
  123.5 158.8 %copy-start.11 = (f32[4096]{0:T(1024)S(1)}, f32[4096]{0:T(1024)}, u32[]{:S(2)}) copy-start(f32[4096]{0:T(1024)} %param.19) | copy-start | bytes 49156
  123.5 188.9 %all-gather.8.cloned.1.call-start = ((), (), s32[]{:S(2)}) async-start(), calls=%async_computation.4 | async-start | bytes 2621440 | tf_op jit(solution)/shard_map/all_gather | solution.py:94
  277.2 5.1 %copy-start.1 = (bf16[2,256,4096]{2,1,0:T(8,128)(2,1)S(1)}, bf16[2,256,4096]{2,1,0:T(8,128)(2,1)}, u32[]{:S(2)}) copy-start(bf16[2,256,4096]{2,1,0:T(8,128)(2,1)} %all-gather.4.cloned.1.call-done) | copy-start | bytes 12582916
  277.2 5.9 %copy-start.2 = (bf16[512,4096]{1,0:T(8,128)(2,1)S(1)}, bf16[512,4096]{1,0:T(8,128)(2,1)}, u32[]{:S(2)}) copy-start(bf16[512,4096]{1,0:T(8,128)(2,1)} %all-reduce.2.cloned.1.call-done) | copy-start | bytes 12582916
  283.1 4.3 %copy-start.15 = (bf16[4096,512]{1,0:T(8,128)(2,1)S(1)}, bf16[4096,512]{1,0:T(8,128)(2,1)}, u32[]{:S(2)}) copy-start(bf16[4096,512]{1,0:T(8,128)(2,1)} %param.20) | copy-start | bytes 12582916
  285.5 1.9 copy-start.7
  290.7 7.0 %copy-start.16 = (s32[8,1]{0,1:T(1,128)S(1)}, s32[8,1]{0,1:T(1,128)}, u32[]{:S(2)}) copy-start(s32[8,1]{0,1:T(1,128)} %param.24) | copy-start | bytes 100
  290.7 7.0 %copy-start.12 = (s32[8]{0:T(128)S(1)}, s32[8]{0:T(128)}, u32[]{:S(2)}) copy-start(s32[8]{0:T(128)} %param.25) | copy-start | bytes 100
  290.7 7.1 %copy-start.8 = (bf16[1,32,512]{2,1,0:T(8,128)(2,1)S(1)}, bf16[1,32,512]{2,1,0:T(8,128)(2,1)}, u32[]{:S(2)}) copy-start(bf16[1,32,512]{2,1,0:T(8,128)(2,1)} %param.23) | copy-start | bytes 98308
  290.7 7.2 %copy-start.9 = (bf16[1,32,512]{2,1,0:T(8,128)(2,1)S(1)}, bf16[1,32,512]{2,1,0:T(8,128)(2,1)}, u32[]{:S(2)}) copy-start(bf16[1,32,512]{2,1,0:T(8,128)(2,1)} %param.22) | copy-start | bytes 98308
  290.7 46.4 %all-gather.6.cloned.1.call-start = ((), (), s32[]{:S(2)}) async-start(), calls=%async_computation.3 | async-start | bytes 2621440 | tf_op jit(solution)/shard_map/all_gather | solution.py:95
  297.4 73.8 %reduce-scatter.2.cloned.1.call-start = ((), (), s32[]{:S(2)}) async-start(), calls=%async_computation.5 | async-start | bytes 2621440 | tf_op jit(solution)/shard_map/reduce_scatter | solution.py:124
  316.0 2.6 copy-start.3
Sparse Core Ops, SparseCore 0:
  9.6 83.4 all-gather.3
  123.7 153.5 all-reduce.1
  290.8 21.5 all-gather.7
  314.5 22.5 all-gather.5
  339.7 31.4 reduce-scatter.1
where the time goes:
time: 380 us
  waiting for transfers between devices  293 us (77%)
  matrix products  36.2 us (10%)
  local copies, waits for them, and re-layouts  21 us (6%)
  other arithmetic  14.7 us (4%)
  between operations  14.1 us (4%)
    psum x1, waiting for transfers between devices, shards(): lax.psum(partial_value.astype(jnp.bfloat16), 'tensor').astype(jnp.float32)  154 us
    all_gather x1, waiting for transfers between devices, shards(): gathered_in = lax.all_gather(tokens, 'tensor', axis=2, tiled=True)  84.3 us
    reduce_scatter x1, waiting for transfers between devices, shards(): lax.psum_scatter(value_term.reshape(token_total, local_cols).astype(jnp.b...  21.7 us
    all_gather x1, waiting for transfers between devices, shards(): lax.all_gather(cross_values, 'dp', axis=0, tiled=True)  18.5 us
    all_gather x1, waiting for transfers between devices, shards(): lax.all_gather(cross_keys, 'dp', axis=0, tiled=True)  14.4 us
    dot_general x3, matrix products, project(): jnp.dot(normed, weight, preferred_element_type=jnp.float32)  11.4 us
    reduce_sum x2, other arithmetic, norm_rows(): jnp.mean(values * values, axis=-1, keepdims=True) + 1e-06  8.26 us
  transfers between devices with their start and end apart: 5, of which 5 were waited for; matrix products, arithmetic and copies ran while one was open for 7% of the time, Pallas kernels for 0%

commit v1 on v0

v1 whole, which is shorter than its diff:
```python
import jax
import jax.numpy as jnp
from jax import lax
from jax.sharding import PartitionSpec as P

HD = 64


blocked = -1e30


def norm_rows(values, gain):
    return values * lax.rsqrt(jnp.mean(values * values, axis=-1, keepdims=True) + 1e-06) * gain


def shards(
    tokens,
    ln_gain,
    w_query,
    w_key,
    w_value,
    w_out,
    final_gain,
    w_cross_key,
    w_cross_value,
    dec_query,
    grad_out,
    passage_query,
    passage_length,
):
    pass_dev, seq_len, part_width = tokens.shape
    local_cols = w_query.shape[1]
    local_heads = local_cols // HD
    score_scale = HD ** (-0.5)
    row_count = pass_dev * seq_len
    query_count = dec_query.shape[0]
    dec_len = dec_query.shape[1]
    slices = lax.axis_size("groups") * lax.axis_size("dp")
    slice_rows = local_cols // slices
    slice_at = lax.axis_index("groups") * lax.axis_size("dp") + lax.axis_index("dp")
    out_slice = lax.dynamic_slice_in_dim(w_out, slice_at * slice_rows, slice_rows, 0)
    out_slice = lax.all_gather(out_slice, "tensor", axis=0, tiled=True)
    out_full = lax.all_gather(out_slice, ("groups", "dp"), axis=0, tiled=True)
    asked = lax.all_gather(jnp.stack([dec_query, grad_out]), "dp", axis=1, tiled=True)
    gathered_in = lax.all_gather(tokens, "tensor", axis=2, tiled=True)
    full_width = gathered_in.shape[2]
    inputs_f = gathered_in.reshape(row_count, full_width).astype(jnp.float32)
    normed = norm_rows(inputs_f, ln_gain).astype(jnp.bfloat16)

    def project(weight):
        return (
            jnp.dot(normed, weight, preferred_element_type=jnp.float32)
            .astype(jnp.bfloat16)
            .reshape(pass_dev, seq_len, local_heads, HD)
        )

    self_queries = project(w_query)
    self_keys = project(w_key)
    self_values = project(w_value)
    pass_start = lax.axis_index("dp") * pass_dev
    own_length = lax.dynamic_slice_in_dim(passage_length, pass_start, pass_dev)
    positions = jnp.arange(seq_len, dtype=jnp.int32)
    own_valid = positions[None, :] < own_length[:, None]
    scores = (
        jnp.einsum("pqhd,pkhd->phqk", self_queries, self_keys, preferred_element_type=jnp.float32)
        * score_scale
    )
    scores = jnp.where(own_valid[:, None, None, :], scores, blocked)
    row_peak = jnp.max(scores, axis=-1, keepdims=True)
    expd = jnp.where(own_valid[:, None, None, :], jnp.exp(scores - row_peak), 0.0)
    weights = (expd / jnp.sum(expd, axis=-1, keepdims=True)).astype(jnp.bfloat16)
    context = (
        jnp.einsum("phqk,pkhd->pqhd", weights, self_values, preferred_element_type=jnp.float32)
        .astype(jnp.bfloat16)
        .reshape(row_count, local_cols)
    )
    all_context = lax.all_gather(context, "tensor", axis=0, tiled=False)
    tensor_count = all_context.shape[0]
    all_context = (
        all_context.reshape(tensor_count, row_count, slices, slice_rows)
        .transpose(1, 2, 0, 3)
        .reshape(row_count, tensor_count * local_cols)
    )
    summed = jnp.dot(all_context, out_full, preferred_element_type=jnp.float32)
    encoded = norm_rows(inputs_f + summed, final_gain).astype(jnp.bfloat16)
    cross_keys = jnp.dot(encoded, w_cross_key, preferred_element_type=jnp.float32).astype(
        jnp.bfloat16
    )
    cross_values = jnp.dot(encoded, w_cross_value, preferred_element_type=jnp.float32).astype(
        jnp.bfloat16
    )
    own_query = lax.dynamic_slice_in_dim(passage_query[:, 0], pass_start, pass_dev)
    chosen = own_query[:, None] == jnp.arange(asked.shape[1], dtype=jnp.int32)[None, :]
    picked = jnp.sum(
        jnp.where(chosen[None, :, :, None, None], asked[:, None].astype(jnp.float32), 0.0), axis=2
    ).astype(jnp.bfloat16)
    picked = picked.reshape(2, pass_dev, dec_len, local_heads, HD)
    query_heads, out_grad = picked[0], picked[1]
    key_heads = cross_keys.reshape(pass_dev, seq_len, local_heads, HD)
    value_heads = cross_values.reshape(pass_dev, seq_len, local_heads, HD)
    key_ok = own_valid[:, None, None, :]
    cross_scores = (
        jnp.einsum("pihd,pthd->phit", query_heads, key_heads, preferred_element_type=jnp.float32)
        * score_scale
    )
    cross_scores = jnp.where(key_ok, cross_scores, blocked)
    own_peak = jnp.max(cross_scores, axis=-1, keepdims=True)
    own_exp = jnp.where(key_ok, jnp.exp(cross_scores - own_peak), 0.0)
    own_sum = jnp.sum(own_exp, axis=-1, keepdims=True)
    own_probs = own_exp / own_sum
    grad_probs = jnp.einsum(
        "pihd,pthd->phit", out_grad, value_heads, preferred_element_type=jnp.float32
    )
    own_delta = jnp.sum(own_probs * grad_probs, axis=-1, keepdims=True)
    stats = jnp.concatenate([own_peak, own_sum, own_delta], axis=-1)
    all_stats = lax.all_gather(stats, "dp", axis=0, tiled=True)
    own_low = own_probs.astype(jnp.bfloat16)
    centred = (own_probs * (grad_probs - own_delta)).astype(jnp.bfloat16)

    def over_keys(factor, heads):
        return jnp.einsum("phit,pthd->pihd", factor, heads, preferred_element_type=jnp.float32)

    partials = jnp.stack(
        [
            over_keys(own_low, value_heads),
            over_keys(centred, key_heads),
            over_keys(own_low, key_heads),
        ],
        axis=1,
    ).astype(jnp.bfloat16)
    partials = partials.reshape(pass_dev, 3, dec_len, local_cols)
    all_partials = lax.all_gather(partials, "dp", axis=0, tiled=True)
    pass_total = all_partials.shape[0]

    def shares(targets):
        owned = (targets[:, None] == passage_query[:, 0][None, :])[:, :, None, None]
        peaks = jnp.where(owned, all_stats[None, :, :, :, 0], blocked)
        top = jnp.max(peaks, axis=1, keepdims=True)
        raised = jnp.where(owned, jnp.exp(peaks - top) , 0.0)
        total = jnp.sum(raised * all_stats[None, :, :, :, 1], axis=1, keepdims=True)
        return raised, total, top

    _, own_total, own_top = shares(own_query)
    low = (
        own_exp * (jnp.exp(own_peak - own_top[:, 0, :, :, None]) / own_total[:, 0, :, :, None])
    ).astype(jnp.bfloat16)
    d_values = jnp.einsum(
        "phit,pihd->pthd", low, out_grad, preferred_element_type=jnp.float32
    ).astype(jnp.bfloat16).reshape(pass_dev, seq_len, local_cols)
    query_ids = lax.axis_index("dp") * query_count + jnp.arange(query_count, dtype=jnp.int32)
    raised, total, _ = shares(query_ids)
    share = raised * all_stats[None, :, :, :, 1] / total
    share = share.transpose(0, 1, 3, 2)[..., None]
    pieces = all_partials.astype(jnp.float32).reshape(
        1, pass_total, 3, dec_len, local_heads, HD
    )
    attended_heads = jnp.sum(share * pieces[:, :, 0], axis=1).astype(jnp.bfloat16)
    grad_heads = grad_out.reshape(query_count, dec_len, local_heads, HD)
    row_delta = jnp.sum(
        grad_heads.astype(jnp.float32) * attended_heads.astype(jnp.float32), axis=-1
    )
    shift = all_stats[None, :, :, :, 2].transpose(0, 1, 3, 2) - row_delta[:, None]
    query_term = jnp.sum(share * (pieces[:, :, 1] + shift[..., None] * pieces[:, :, 2]), axis=1)
    attended = attended_heads.reshape(query_count, dec_len, local_cols)
    d_query = (
        (query_term * score_scale).astype(jnp.bfloat16).reshape(query_count, dec_len, local_cols)
    )
    return (attended, d_query, d_values)


def solution(mesh):
    in_specs = (
        P(("groups", "dp"), None, "tensor"),
        P(),
        P(None, "tensor"),
        P(None, "tensor"),
        P(None, "tensor"),
        P("tensor", None),
        P(),
        P(None, "tensor"),
        P(None, "tensor"),
        P(("groups", "dp"), None, "tensor"),
        P(("groups", "dp"), None, "tensor"),
        P("groups", None),
        P("groups"),
    )
    out_specs = (
        P(("groups", "dp"), None, "tensor"),
        P(("groups", "dp"), None, "tensor"),
        P(("groups", "dp"), None, "tensor"),
    )
    return jax.shard_map(shards, mesh=mesh, in_specs=in_specs, out_specs=out_specs, check_vma=False)
```

time: 380 us -> 340 us (0.89)
  waiting for transfers between devices: 293 us -> 225 us
  blocking collectives: 0 us -> 20.7 us
  matrix products: 36.2 us -> 44.3 us
  local copies, waits for them, and re-layouts: 21 us -> 25.9 us
  other arithmetic: 14.7 us -> 9.91 us
    psum x1 -> x0, waiting for transfers between devices: 154 us -> none  [shards(): lax.psum(partial_value.astype(jnp.bfloat16), 'tensor').astype(jnp.float32)]
    all_gather x2 -> x3, waiting for transfers between devices: 32.9 us -> 142 us  [the longest x1 86 us: shards(): out_full = lax.all_gather(out_slice, ('groups', 'dp'), axis=0, tiled=True)]
    reduce_scatter x1 -> x0, waiting for transfers between devices: 21.7 us -> none  [shards(): lax.psum_scatter(value_term.reshape(token_total, local_cols).astype(jnp.b...]
    all_gather x0 -> x3, blocking collectives: none -> 20.7 us  [the longest x1 9.17 us: shards(): all_partials = lax.all_gather(partials, 'dp', axis=0, tiled=True)]
    dot_general x5 -> x7, matrix products: 13.8 us -> 19.1 us  [the longest x1 15.1 us: shards(): summed = jnp.dot(all_context, out_full, preferred_element_type=jnp.float32)]
    reduce_sum x2 -> x1, other arithmetic: 8.26 us -> 3.23 us  [norm_rows(): jnp.mean(values * values, axis=-1, keepdims=True) + 1e-06]
    dot_general x1, matrix products: 6.59 us -> 2.37 us  [shards(): jnp.dot(encoded, w_cross_value, preferred_element_type=jnp.float32)]
    all_gather x2 -> x1, local copies, waits for them, and re-layouts: 6.89 us -> 2.79 us  [shards(): all_context = lax.all_gather(context, 'tensor', axis=0, tiled=False)]
  transfers between devices with their start and end apart: 5 -> 4, of which waited for: 5 -> 4; matrix products, arithmetic and copies ran while one was open for 7% -> 11% of each run, Pallas kernels for 0% -> 0%
where the time goes in v1:
time: 340 us
  waiting for transfers between devices  225 us (66%)
  matrix products  44.3 us (13%)
  local copies, waits for them, and re-layouts  25.9 us (8%)
  blocking collectives  20.7 us (6%)
  between operations  14.2 us (4%)
  other arithmetic  9.91 us (3%)
    all_gather x1, waiting for transfers between devices, shards(): out_full = lax.all_gather(out_slice, ('groups', 'dp'), axis=0, tiled=True)  86 us
    all_gather x1, waiting for transfers between devices, shards(): gathered_in = lax.all_gather(tokens, 'tensor', axis=2, tiled=True)  82.4 us
    all_gather x1, waiting for transfers between devices, shards(): all_context = lax.all_gather(context, 'tensor', axis=0, tiled=False)  39.3 us
    all_gather x1, waiting for transfers between devices, shards(): out_slice = lax.all_gather(out_slice, 'tensor', axis=0, tiled=True)  16.5 us
    dot_general x1, matrix products, shards(): summed = jnp.dot(all_context, out_full, preferred_element_type=jnp.float32)  15.1 us
    dot_general x3, matrix products, project(): jnp.dot(normed, weight, preferred_element_type=jnp.float32)  14.7 us
    all_gather x1, blocking collectives, shards(): all_partials = lax.all_gather(partials, 'dp', axis=0, tiled=True)  9.17 us
    dot_general x1, matrix products, shards(): jnp.dot(encoded, w_cross_key, preferred_element_type=jnp.float32)  6.94 us
  transfers between devices with their start and end apart: 4, of which 4 were waited for; matrix products, arithmetic and copies ran while one was open for 11% of the time, Pallas kernels for 0%

profile of v1, /device:TPU:0, one launch (start us, length us, event | category | flops | bytes accessed | tf_op | source)
XLA Modules:
  0.0 340.1 jit_solution(8476776203954746965)
XLA Ops:
  7.2 0.7 all-gather.5.cloned.1.call-update
  8.0 1.9 constant_dynamic-slice_fusion
  9.9 0.7 dynamic_slice.9
  10.7 82.4 %all-gather.5.cloned.1.call-done = bf16[2,256,4096]{2,1,0:T(8,128)(2,1)} async-done(((bf16[2,256,1024]{2,1,0:T(8,128)(2,1)}), bf16[2,256,4096]{2,1,0:T(8,128)(2,1)}) %all-gather.5.cloned.1.call-update) | async-done | bytes 4194320 | tf_op jit(solution)/shard_map/all_gather | solution.py:45
  93.1 3.2 fusion.1
  96.5 1.7 fusion.3
  98.2 1.9 copy-done.1
  100.1 2.3 convolution_convert_fusion.3
  102.5 0.5 reshape.390
  103.0 5.8 %convolution_convert_fusion.2 = bf16[512,512]{1,0:T(8,128)(2,1)S(1)} fusion(bf16[512,4096]{1,0:T(8,128)(2,1)} %copy-done.1, bf16[4096,512]{1,0:T(8,128)(2,1)} %param.16), kind=kOutput, calls=%fused_computation.19 | convolution fusion | flops 2147745792 | bytes 8912896 | tf_op jit(solution)/shard_map/dot_general | solution.py:52
  108.8 0.5 reshape.391
  109.3 6.6 %convolution_convert_fusion.4 = bf16[512,512]{1,0:T(8,128)(2,1)} fusion(bf16[512,4096]{1,0:T(8,128)(2,1)} %copy-done.1, bf16[4096,512]{1,0:T(8,128)(2,1)} %param.17), kind=kOutput, calls=%fused_computation.21 | convolution fusion | flops 2147745792 | bytes 8912896 | tf_op jit(solution)/shard_map/dot_general | solution.py:52
  115.9 1.6 reshape.389
  117.6 0.7 fusion.21
  118.3 1.7 fusion.54
  120.1 0.5 fusion.10
  120.6 0.6 copy.116
  121.2 1.4 reshape.392
  122.7 16.5 %all-gather.9.cloned.1.call-done = bf16[256,4096]{1,0:T(8,128)(2,1)} async-done(((bf16[64,4096]{1,0:T(8,128)(2,1)}), bf16[256,4096]{1,0:T(8,128)(2,1)}) %all-gather.9.cloned.1.call-update) | async-done | bytes 2097168 | tf_op jit(solution)/shard_map/all_gather | solution.py:42
  139.2 0.8 reshape.387
  139.9 6.0 %all_gather.21 = bf16[2,4,32,512]{3,2,1,0:T(8,128)(2,1)S(1)} all-gather(bf16[2,1,32,512]{3,2,1,0:T(8,128)(2,1)S(1)} %pad_maximum_fusion.1), channel_id=1, replica_groups=mesh['groups'=2,'dp'=4,'tensor'=4] {'dp'}, dimensions={1}, use_global_device_ids=true | all-gather | bytes 327680 | tf_op jit(solution)/shard_map/all_gather | solution.py:44
  146.7 39.3 %all-gather.7.cloned.1.call-done = bf16[4,512,512]{2,1,0:T(8,128)(2,1)} async-done(((bf16[1,512,512]{2,1,0:T(8,128)(2,1)}), bf16[4,512,512]{2,1,0:T(8,128)(2,1)}) %all-gather.7.cloned.1.call-update) | async-done | bytes 2097168 | tf_op jit(solution)/shard_map/all_gather | solution.py:77
  185.9 2.8 copy.90
  188.7 1.5 copy.91
  190.2 86.0 %all-gather.11.cloned.1.call-done = bf16[2048,4096]{1,0:T(8,128)(2,1)} async-done(((bf16[256,4096]{1,0:T(8,128)(2,1)}), bf16[2048,4096]{1,0:T(8,128)(2,1)}) %all-gather.11.cloned.1.call-update) | async-done | bytes 16777232 | tf_op jit(solution)/shard_map/all_gather | solution.py:43
  276.3 15.1 %multiply_reduce_fusion = (f32[512]{0:T(512)S(1)}, f32[512,4096]{1,0:T(8,128)S(1)}) fusion(bf16[512,2048]{0,1:T(8,128)(2,1)} %bitcast.123, bf16[2048,4096]{1,0:T(8,128)(2,1)} %all-gather.11.cloned.1.call-done, bf16[2,256,4096]{2,1,0:T(8,128)(2,1)} %all-gather.5.cloned.1.call-done), kind=kOutput, calls=%fused_computation.8 | convolution fusion | flops 8598323200 | bytes 31459328 | tf_op jit(solution)/shard_map/dot_general | solution.py:84
  291.4 3.2 copy-done.9
  294.7 2.4 convolution_convert_fusion
  297.0 0.5 reshape.394
  297.6 0.6 copy.97
  298.2 6.9 %convolution_convert_fusion.1 = bf16[512,512]{1,0:T(8,128)(2,1)S(1)} fusion(bf16[4096,512]{1,0:T(8,128)(2,1)} %param.20, f32[512,4096]{1,0:T(8,128)} %copy-done.9, f32[4096]{0:T(1024)S(1)} %copy-done.7, f32[512]{0:T(512)S(1)} %add_rsqrt_fusion), kind=kOutput, calls=%fused_computation.18 | convolution fusion | flops 2154037248 | bytes 13125632 | tf_op jit(solution)/shard_map/dot_general | solution.py:86
  305.1 0.5 reshape.393
  305.7 0.6 copy.94
  306.3 0.3 fusion.55
  306.8 0.3 fusion.14
  307.2 0.3 fusion.12
  307.5 1.0 multiply_reduce_fusion.1
  308.5 5.5 %all_gather.26 = f32[8,8,32,3]{2,1,0,3:T(8,128)S(1)} all-gather(f32[2,8,32,3]{2,1,0,3:T(8,128)S(1)} %pad_maximum_fusion.2), channel_id=1, replica_groups=mesh['groups'=2,'dp'=4,'tensor'=4] {'dp'}, dimensions={0}, use_global_device_ids=true | all-gather | bytes 30720 | tf_op jit(solution)/shard_map/all_gather | solution.py:116
  314.3 0.5 convolution_convert_fusion.5
  314.8 1.0 copy.108
  316.4 1.4 fusion.13
  318.3 9.2 %all_gather.27 = bf16[8,3,32,512]{3,2,0,1:T(8,128)(2,1)} all-gather(bf16[2,3,32,512]{3,2,0,1:T(8,128)(2,1)S(1)} %pad_maximum_fusion), channel_id=1, replica_groups=mesh['groups'=2,'dp'=4,'tensor'=4] {'dp'}, dimensions={0}, use_global_device_ids=true | all-gather | bytes 983040 | tf_op jit(solution)/shard_map/all_gather | solution.py:132
  327.4 2.3 reshape.386
  329.8 0.3 fusion.20
  330.1 0.7 convert_element_type.157
  330.9 1.0 fusion.32
  332.1 0.7 fusion.18
  332.8 0.7 convert_element_type.163
  (60 shorter events, 2.9 us)
Async XLA Ops:
  7.2 89.2 %copy-start.4 = (f32[4096]{0:T(1024)S(1)}, f32[4096]{0:T(1024)}, u32[]{:S(2)}) copy-start(f32[4096]{0:T(1024)} %param.14) | copy-start | bytes 49156
  7.2 85.9 %all-gather.5.cloned.1.call-start = ((), (), s32[]{:S(2)}) async-start(), calls=%async_computation | async-start | bytes 5242880 | tf_op jit(solution)/shard_map/all_gather | solution.py:45
  7.9 131.2 %all-gather.9.cloned.1.call-start = ((), (), s32[]{:S(2)}) async-start(), calls=%async_computation.2 | async-start | bytes 2621440 | tf_op jit(solution)/shard_map/all_gather | solution.py:42
  9.9 176.1 %all-gather.7.cloned.1.call-start = ((), (), s32[]{:S(2)}) async-start(), calls=%async_computation.1 | async-start | bytes 2621440 | tf_op jit(solution)/shard_map/all_gather | solution.py:77
  93.1 3.4 %copy-start = (bf16[2,256,4096]{2,1,0:T(8,128)(2,1)S(1)}, bf16[2,256,4096]{2,1,0:T(8,128)(2,1)}, u32[]{:S(2)}) copy-start(bf16[2,256,4096]{2,1,0:T(8,128)(2,1)} %all-gather.5.cloned.1.call-done) | copy-start | bytes 12582916
  96.5 3.6 %copy-start.5 = (bf16[4096,512]{1,0:T(8,128)(2,1)S(1)}, bf16[4096,512]{1,0:T(8,128)(2,1)}, u32[]{:S(2)}) copy-start(bf16[4096,512]{1,0:T(8,128)(2,1)} %param.15) | copy-start | bytes 12582916
  98.2 1.9 copy-start.1
  120.6 18.6 %copy-start.2 = (bf16[1,32,512]{2,1,0:T(8,128)(2,1)S(1)}, bf16[1,32,512]{2,1,0:T(8,128)(2,1)}, u32[]{:S(2)}) copy-start(bf16[1,32,512]{2,1,0:T(8,128)(2,1)} %param.23) | copy-start | bytes 98308
  120.6 19.3 %copy-start.3 = (bf16[1,32,512]{2,1,0:T(8,128)(2,1)S(1)}, bf16[1,32,512]{2,1,0:T(8,128)(2,1)}, u32[]{:S(2)}) copy-start(bf16[1,32,512]{2,1,0:T(8,128)(2,1)} %param.22) | copy-start | bytes 98308
  120.6 25.4 %copy-start.8 = (s32[8,1]{0,1:T(1,128)S(1)}, s32[8,1]{0,1:T(1,128)}, u32[]{:S(2)}) copy-start(s32[8,1]{0,1:T(1,128)} %param.24) | copy-start | bytes 100
  122.6 153.6 %all-gather.11.cloned.1.call-start = ((), (), s32[]{:S(2)}) async-start(), calls=%async_computation.3 | async-start | bytes 18874368 | tf_op jit(solution)/shard_map/all_gather | solution.py:43
  276.3 18.4 %copy-start.6 = (bf16[4096,512]{1,0:T(8,128)(2,1)S(1)}, bf16[4096,512]{1,0:T(8,128)(2,1)}, u32[]{:S(2)}) copy-start(bf16[4096,512]{1,0:T(8,128)(2,1)} %param.21) | copy-start | bytes 12582916
  276.3 18.4 %copy-start.7 = (f32[4096]{0:T(1024)S(1)}, f32[4096]{0:T(1024)}, u32[]{:S(2)}) copy-start(f32[4096]{0:T(1024)} %param.19) | copy-start | bytes 49156
  291.4 3.2 copy-start.9
Sparse Core Ops, SparseCore 0:
  9.6 83.4 all-gather.4
  94.6 44.4 all-gather.8
  141.3 44.5 all-gather.6
  187.7 88.5 all-gather.10

commit v2 on v1

--- a/solution.py
+++ b/solution.py
@@ -1,6 +1,10 @@
+import functools
+
 import jax
 import jax.numpy as jnp
 from jax import lax
+from jax.experimental import pallas as pl
+from jax.experimental.pallas import tpu as pltpu
 from jax.sharding import PartitionSpec as P
 
 HD = 64
@@ -11,6 +15,288 @@
 
 def norm_rows(values, gain):
     return values * lax.rsqrt(jnp.mean(values * values, axis=-1, keepdims=True) + 1e-06) * gain
+
+
+MESH = pl.DeviceIdType.MESH
+
+
+def remote(src, dst, send_sem, recv_sem, target):
+    return pltpu.make_async_remote_copy(
+        src_ref=src,
+        dst_ref=dst,
+        send_sem=send_sem,
+        recv_sem=recv_sem,
+        device_id=target,
+        device_id_type=MESH,
+    )
+
+
+def greet(targets, conditions):
+    barrier = pltpu.get_barrier_semaphore()
+    amount = 0
+    for target, condition in zip(targets, conditions):
+        if condition is None:
+            pl.semaphore_signal(barrier, inc=1, device_id=target, device_id_type=MESH)
+            amount = amount + 1
+        else:
+
+            @pl.when(condition)
+            def _(target=target):
+                pl.semaphore_signal(barrier, inc=1, device_id=target, device_id_type=MESH)
+
+            amount = amount + condition.astype(jnp.int32)
+    pl.semaphore_wait(barrier, amount)
+
+
+class Chain:
+    def __init__(self, count, place, own, block, send_sem, recv_sem):
+        self.count, self.place, self.own, self.block = count, place, own, block
+        self.send_sem, self.recv_sem = send_sem, recv_sem
+
+    def arriving(self, step, way):
+        index = self.place - 1 - step if way == 0 else self.place + 1 + step
+        return index, (index >= 0 if way == 0 else index < self.count)
+
+    def onward(self, way):
+        target = self.place + 1 if way == 0 else self.place - 1
+        return target, (target < self.count if way == 0 else target >= 0)
+
+    def copy(self, step, way, index, src=None):
+        block = self.block(index)
+        target, _ = self.onward(way)
+        slot = 2 * step + way
+        return remote(
+            block if src is None else src,
+            block,
+            self.send_sem.at[slot],
+            self.recv_sem.at[slot],
+            {"tensor": target},
+        )
+
+    def begin(self):
+        for way in range(2):
+
+            @pl.when(self.onward(way)[1])
+            def _(way=way):
+                self.copy(0, way, self.place, self.own).start()
+
+    def receive(self, step, way):
+        index, _ = self.arriving(step, way)
+        self.copy(step, way, index).wait_recv()
+        if step + 1 < self.count - 1:
+
+            @pl.when(self.onward(way)[1])
+            def _():
+                self.copy(step + 1, way, index).start()
+
+    def finish(self):
+        for step in range(self.count - 1):
+            for way in range(2):
+                index = self.place - step if way == 0 else self.place + step
+                there = index >= 0 if way == 0 else index < self.count
+
+                @pl.when(there & self.onward(way)[1])
+                def _(step=step, way=way, index=index):
+                    self.copy(step, way, index, self.own if step == 0 else None).wait_send()
+
+
+def columns(ref, index, width):
+    return ref.at[:, pl.ds(pl.multiple_of(index * width, width), width)]
+
+
+def line_targets(count, place):
+    return [{"tensor": place + 1}, {"tensor": place - 1}], [place + 1 < count, place >= 1]
+
+
+def line_kernel(count, x_ref, out_ref, local_sem, send_sem, recv_sem):
+    place = lax.axis_index("tensor")
+    width = x_ref.shape[1]
+    keep = pltpu.make_async_copy(x_ref, columns(out_ref, place, width), local_sem)
+    keep.start()
+    greet(*line_targets(count, place))
+    chain = Chain(
+        count, place, x_ref, lambda index: columns(out_ref, index, width), send_sem, recv_sem
+    )
+    chain.begin()
+    for step in range(count - 1):
+        for way in range(2):
+
+            @pl.when(chain.arriving(step, way)[1])
+            def _(step=step, way=way):
+                chain.receive(step, way)
+
+    chain.finish()
+    keep.wait()
+
+
+def line_gather(x, count):
+    slots = 2 * (count - 1)
+    return pl.pallas_call(
+        functools.partial(line_kernel, count),
+        out_shape=jax.ShapeDtypeStruct((x.shape[0], x.shape[1] * count), x.dtype),
+        in_specs=[pl.BlockSpec(memory_space=pl.ANY)],
+        out_specs=pl.BlockSpec(memory_space=pl.ANY),
+        scratch_shapes=[
+            pltpu.SemaphoreType.DMA,
+            pltpu.SemaphoreType.DMA((slots,)),
+            pltpu.SemaphoreType.DMA((slots,)),
+        ],
+        compiler_params=pltpu.CompilerParams(collective_id=1, has_side_effects=True),
+    )(x)
+
+
+def spread_kernel(
+    sizes,
+    tok_ref,
+    w_ref,
+    tok_out,
+    w_out,
+    local_sem,
+    tok_send,
+    tok_recv,
+    w_send,
+    w_recv,
+    g_send,
+    g_recv,
+    y_send,
+    y_recv,
+    c_send,
+    c_recv,
+):
+    groups, rows, count = sizes
+    group, dp, place = (lax.axis_index(name) for name in ("groups", "dp", "tensor"))
+    row, core = lax.div(dp, 2), lax.rem(dp, 2)
+    width = tok_ref.shape[1]
+    keeps = (
+        pltpu.make_async_copy(tok_ref, columns(tok_out, place, width), local_sem.at[0]),
+        pltpu.make_async_copy(w_ref, w_out.at[place], local_sem.at[1]),
+    )
+    for keep in keeps:
+        keep.start()
+    other_groups = [lax.rem(group + hop, groups) for hop in range(groups)]
+    other_rows = [lax.rem(row + hop, rows) for hop in range(rows)]
+    sibling = {"dp": row * 2 + 1 - core}
+    targets, conditions = line_targets(count, place)
+    targets += [{"groups": g} for g in other_groups[1:]]
+    targets += [{"dp": y * 2 + core} for y in other_rows[1:]] + [sibling]
+    greet(targets, conditions + [None] * (groups + rows - 1))
+
+    def at(group_at, row_at, core_at):
+        return (group_at * rows + row_at) * 2 + core_at
+
+    mine = at(group, row, core)
+    weights = Chain(
+        count, place, w_ref.at[mine], lambda index: w_out.at[index, mine], w_send, w_recv
+    )
+    toks = Chain(
+        count, place, tok_ref, lambda index: columns(tok_out, index, width), tok_send, tok_recv
+    )
+
+    def across(step, way, hop, outward):
+        index, slot = weights.arriving(step, way)[0], 2 * step + way
+        sems = g_send.at[slot, hop - 1], g_recv.at[slot, hop - 1]
+        there = w_out.at[index, mine]
+        source = at(other_groups[groups - hop], row, core)
+        here = w_out.at[index, source]
+        target = {"groups": other_groups[hop]}
+        block = there if outward else here
+        return remote(block, block, *sems, target)
+
+    def along(step, way, hop_g, hop, outward):
+        index, slot = weights.arriving(step, way)[0], 2 * step + way
+        sems = y_send.at[slot, hop_g, hop - 1], y_recv.at[slot, hop_g, hop - 1]
+        block_group = other_groups[(groups - hop_g) % groups]
+        there = w_out.at[index, at(block_group, row, core)]
+        here = w_out.at[index, at(block_group, other_rows[rows - hop], core)]
+        target = {"dp": other_rows[hop] * 2 + core}
+        block = there if outward else here
+        return remote(block, block, *sems, target)
+
+    def beside(step, way, hop_g, hop, outward):
+        index, slot = weights.arriving(step, way)[0], 2 * step + way
+        sems = c_send.at[slot, hop_g, hop], c_recv.at[slot, hop_g, hop]
+        block_group = other_groups[(groups - hop_g) % groups]
+        block_row = other_rows[(rows - hop) % rows]
+        there = w_out.at[index, at(block_group, block_row, core)]
+        here = w_out.at[index, at(block_group, block_row, 1 - core)]
+        block = there if outward else here
+        return remote(block, block, *sems, sibling)
+
+    def first(step, way):
+        weights.receive(step, way)
+        for hop in range(1, groups):
+            across(step, way, hop, True).start()
+        for hop in range(1, rows):
+            along(step, way, 0, hop, True).start()
+        beside(step, way, 0, 0, True).start()
+
+    def second(step, way):
+        for hop_g in range(1, groups):
+            across(step, way, hop_g, False).wait_recv()
+            for hop in range(1, rows):
+                along(step, way, hop_g, hop, True).start()
+            beside(step, way, hop_g, 0, True).start()
+
+    def third(step, way):
+        for hop_g in range(groups):
+            for hop in range(1, rows):
+                along(step, way, hop_g, hop, False).wait_recv()
+                beside(step, way, hop_g, hop, True).start()
+
+    def last(step, way):
+        for hop_g in range(groups):
+            for hop in range(rows):
+                beside(step, way, hop_g, hop, False).wait_recv()
+        for hop in range(1, groups):
+            across(step, way, hop, True).wait_send()
+        for hop_g in range(groups):
+            for hop in range(1, rows):
+                along(step, way, hop_g, hop, True).wait_send()
+            for hop in range(rows):
+                beside(step, way, hop_g, hop, True).wait_send()
+
+    def each_way(step, act):
+        for way in range(2):
+
+            @pl.when(weights.arriving(step, way)[1])
+            def _(way=way):
+                act(step, way)
+
+    weights.begin()
+    toks.begin()
+    for step in range(count - 1):
+        each_way(step, first)
+        if step >= 1:
+            each_way(step - 1, second)
+        each_way(step, toks.receive)
+        if step >= 1:
+            each_way(step - 1, third)
+    each_way(count - 2, second)
+    each_way(count - 2, third)
+    for step in range(count - 1):
+        each_way(step, last)
+    weights.finish()
+    toks.finish()
+    for keep in keeps:
+        keep.wait()
+
+
+def spread(tokens, w_slices, groups, rows, count):
+    slots = 2 * (count - 1)
+    sems = [(slots,), (slots,), (slots, groups - 1), (slots, groups, rows - 1)]
+    sems.append((slots, groups, rows))
+    return pl.pallas_call(
+        functools.partial(spread_kernel, (groups, rows, count)),
+        out_shape=(
+            jax.ShapeDtypeStruct((tokens.shape[0], tokens.shape[1] * count), tokens.dtype),
+            jax.ShapeDtypeStruct((count,) + w_slices.shape, w_slices.dtype),
+        ),
+        in_specs=[pl.BlockSpec(memory_space=pl.ANY)] * 2,
+        out_specs=(pl.BlockSpec(memory_space=pl.ANY),) * 2,
+        scratch_shapes=[pltpu.SemaphoreType.DMA((2,))]
+        + [pltpu.SemaphoreType.DMA(shape) for shape in sems for _ in range(2)],
+        compiler_params=pltpu.CompilerParams(collective_id=0, has_side_effects=True),
+    )(tokens, w_slices)
 
 
 def shards(
@@ -35,15 +321,18 @@
     row_count = pass_dev * seq_len
     query_count = dec_query.shape[0]
     dec_len = dec_query.shape[1]
-    slices = lax.axis_size("groups") * lax.axis_size("dp")
-    slice_rows = local_cols // slices
-    slice_at = lax.axis_index("groups") * lax.axis_size("dp") + lax.axis_index("dp")
-    out_slice = lax.dynamic_slice_in_dim(w_out, slice_at * slice_rows, slice_rows, 0)
-    out_slice = lax.all_gather(out_slice, "tensor", axis=0, tiled=True)
-    out_full = lax.all_gather(out_slice, ("groups", "dp"), axis=0, tiled=True)
+    groups, dp_count = lax.axis_size("groups"), lax.axis_size("dp")
+    tensor_count = lax.axis_size("tensor")
     asked = lax.all_gather(jnp.stack([dec_query, grad_out]), "dp", axis=1, tiled=True)
-    gathered_in = lax.all_gather(tokens, "tensor", axis=2, tiled=True)
-    full_width = gathered_in.shape[2]
+    gathered_in, out_full = spread(
+        tokens.reshape(row_count, part_width),
+        w_out.reshape(groups * dp_count, local_cols // (groups * dp_count), w_out.shape[1]),
+        groups,
+        dp_count // 2,
+        tensor_count,
+    )
+    full_width = gathered_in.shape[1]
+    out_full = out_full.reshape(tensor_count * local_cols, full_width)
     inputs_f = gathered_in.reshape(row_count, full_width).astype(jnp.float32)
     normed = norm_rows(inputs_f, ln_gain).astype(jnp.bfloat16)
 
@@ -74,13 +363,7 @@
         .astype(jnp.bfloat16)
         .reshape(row_count, local_cols)
     )
-    all_context = lax.all_gather(context, "tensor", axis=0, tiled=False)
-    tensor_count = all_context.shape[0]
-    all_context = (
-        all_context.reshape(tensor_count, row_count, slices, slice_rows)
-        .transpose(1, 2, 0, 3)
-        .reshape(row_count, tensor_count * local_cols)
-    )
+    all_context = line_gather(context, tensor_count)
     summed = jnp.dot(all_context, out_full, preferred_element_type=jnp.float32)
     encoded = norm_rows(inputs_f + summed, final_gain).astype(jnp.bfloat16)
     cross_keys = jnp.dot(encoded, w_cross_key, preferred_element_type=jnp.float32).astype(

time: 340 us -> 299 us (0.88)
  waiting for transfers between devices: 225 us -> 0 us
  Pallas kernels: 0 us -> 202 us
  between operations: 14.2 us -> 1.05 us
  local copies, waits for them, and re-layouts: 25.9 us -> 16.9 us
  other arithmetic: 9.91 us -> 14.6 us
    all_gather x4 -> x0, waiting for transfers between devices: 224 us -> none  [the longest x1 86 us: shards(): out_full = lax.all_gather(out_slice, ('groups', 'dp'), axis=0, tiled=True)]
    pallas_call x0 -> x2, Pallas kernels: none -> 202 us  [the longest x1 161 us: spread(): pl.pallas_call(functools.partial(spread_kernel, (groups, rows, count)), o...]
    sub x1, other arithmetic: 1.74 us -> 7.21 us  [shards(): scores - row_peak]
  transfers between devices with their start and end apart: 4 -> 0, of which waited for: 4 -> 0; matrix products, arithmetic and copies ran while one was open for 11% -> 0% of each run, Pallas kernels for 0% -> 0%
where the time goes in v2:
time: 299 us
  Pallas kernels  202 us (68%)
  matrix products  43.7 us (15%)
  blocking collectives  20.5 us (7%)
  local copies, waits for them, and re-layouts  16.9 us (6%)
  other arithmetic  14.6 us (5%)
    pallas_call x1, Pallas kernels, spread(): pl.pallas_call(functools.partial(spread_kernel, (groups, rows, count)), o...  161 us
    pallas_call x1, Pallas kernels, line_gather(): pl.pallas_call(functools.partial(line_kernel, count), out_shape=jax.Shape...  40.9 us
    dot_general x1, matrix products, shards(): summed = jnp.dot(all_context, out_full, preferred_element_type=jnp.float32)  14 us
    dot_general x3, matrix products, project(): jnp.dot(normed, weight, preferred_element_type=jnp.float32)  12.8 us
    all_gather x1, blocking collectives, shards(): all_partials = lax.all_gather(partials, 'dp', axis=0, tiled=True)  9.17 us
    sub x1, other arithmetic, shards(): scores - row_peak  7.21 us
    dot_general x1, matrix products, shards(): jnp.dot(encoded, w_cross_key, preferred_element_type=jnp.float32)  6.96 us

profile of v2, /device:TPU:0, one launch (start us, length us, event | category | flops | bytes accessed | tf_op | source)
XLA Modules:
  0.0 298.6 jit_solution(7091000151724857592)
XLA Ops:
  0.6 160.9 %shard_map.148 = (bf16[512,4096]{1,0:T(8,128)(2,1)}, bf16[4,8,64,4096]{3,2,1,0:T(8,128)(2,1)}) custom-call(bf16[512,1024]{1,0:T(8,128)(2,1)} %bitcast.110, bf16[8,64,4096]{2,1,0:T(8,128)(2,1)} %bitcast.108), custom_call_target="tpu_custom_call" | custom-call | tf_op jit(solution)/shard_map/pallas_call | solution.py:288
  161.6 3.2 %fusion.1 = f32[512]{0:T(512)S(1)} fusion(bf16[512,4096]{1,0:T(8,128)(2,1)} %get-tuple-element.5), kind=kLoop, calls=%fused_computation.4 | loop fusion | flops 6290944 | bytes 4196352 | tf_op jit(solution)/shard_map/reduce_sum | solution.py:17
  164.8 0.2 copy-done
  165.0 4.6 %convolution_convert_fusion.3 = bf16[512,512]{1,0:T(8,128)(2,1)S(1)} fusion(bf16[4096,512]{1,0:T(8,128)(2,1)} %param.15, bf16[512,4096]{1,0:T(8,128)(2,1)S(1)} %copy-done, f32[4096]{0:T(1024)S(1)} %copy-done.6, f32[512]{0:T(512)S(1)} %add_rsqrt_fusion.1), kind=kOutput, calls=%fused_computation.20 | convolution fusion | flops 2156134400 | bytes 8931328 | tf_op jit(solution)/shard_map/dot_general | solution.py:341
  169.6 0.5 reshape.385
  170.1 5.8 %convolution_convert_fusion.2 = bf16[512,512]{1,0:T(8,128)(2,1)S(1)} fusion(bf16[4096,512]{1,0:T(8,128)(2,1)} %param.16, bf16[512,4096]{1,0:T(8,128)(2,1)} %get-tuple-element.5, f32[4096]{0:T(1024)S(1)} %copy-done.6, f32[512]{0:T(512)S(1)} %add_rsqrt_fusion.1), kind=kOutput, calls=%fused_computation.19 | convolution fusion | flops 2156134400 | bytes 8931328 | tf_op jit(solution)/shard_map/dot_general | solution.py:341
  176.0 0.5 reshape.386
  176.5 2.7 fusion.21
  179.4 7.2 %fusion.57 = (f32[2,8,256]{2,1,0:T(8,128)S(1)}, f32[2,8,256,256]{2,3,1,0:T(8,128)}) fusion(f32[2,8,256,256]{2,3,1,0:T(8,128)} %fusion.21, pred[2,256]{1,0:T(4,128)(4,1)S(1)} %iota_compare_fusion), kind=kOutput, calls=%fused_computation.98 | output fusion | flops 7340287 | bytes 8405504 | tf_op jit(solution)/shard_map/sub | solution.py:359
  186.6 2.4 convolution_convert_fusion.4
  189.0 0.5 reshape.384
  189.5 2.7 fusion.10
  192.3 0.7 copy.113
  193.0 1.4 reshape.387.x_ref
  194.4 40.9 %shard_map.149 = bf16[512,2048]{1,0:T(8,128)(2,1)} custom-call(bf16[512,512]{1,0:T(8,128)(2,1)} %reshape.387.x_ref), custom_call_target="tpu_custom_call" | custom-call | tf_op jit(solution)/shard_map/pallas_call | solution.py:134
  235.3 14.0 %multiply_reduce_fusion = (f32[512]{0:T(512)S(1)}, f32[512,4096]{1,0:T(8,128)S(1)}) fusion(bf16[512,2048]{1,0:T(8,128)(2,1)} %shard_map.149, bf16[2048,4096]{1,0:T(8,128)(2,1)} %bitcast.116, bf16[512,4096]{1,0:T(8,128)(2,1)} %get-tuple-element.5), kind=kOutput, calls=%fused_computation.8 | convolution fusion | flops 8598323200 | bytes 31459328 | tf_op jit(solution)/shard_map/dot_general | solution.py:367
  249.4 3.2 %copy-done.10 = f32[512,4096]{1,0:T(8,128)} copy-done((f32[512,4096]{1,0:T(8,128)}, f32[512,4096]{1,0:T(8,128)S(1)}, u32[]{:S(2)}) %copy-start.10) | copy-done | bytes 8388632
  252.6 2.4 convolution_convert_fusion
  255.0 0.5 reshape.389
  255.5 0.6 copy.94
  256.2 7.0 %convolution_convert_fusion.1 = bf16[512,512]{1,0:T(8,128)(2,1)S(1)} fusion(bf16[4096,512]{1,0:T(8,128)(2,1)} %param.20, f32[512,4096]{1,0:T(8,128)} %copy-done.10, f32[4096]{0:T(1024)S(1)} %copy-done.7, f32[512]{0:T(512)S(1)} %add_rsqrt_fusion), kind=kOutput, calls=%fused_computation.18 | convolution fusion | flops 2154037248 | bytes 13125632 | tf_op jit(solution)/shard_map/dot_general | solution.py:369
  263.1 0.5 reshape.388
  263.7 0.6 copy.91
  264.4 5.8 %all_gather.9 = bf16[2,4,32,512]{3,2,1,0:T(8,128)(2,1)S(1)} all-gather(bf16[2,1,32,512]{3,2,1,0:T(8,128)(2,1)S(1)} %pad_maximum_fusion.1), channel_id=1, replica_groups=mesh['groups'=2,'dp'=4,'tensor'=4] {'dp'}, dimensions={1}, use_global_device_ids=true | all-gather | bytes 327680 | tf_op jit(solution)/shard_map/all_gather | solution.py:326
  270.3 0.1 select_reduce_fusion
  270.5 0.1 squeeze.16
  270.6 0.3 fusion.58
  270.9 0.3 fusion.26
  271.2 0.1 squeeze.17
  271.3 0.3 multiply_reduce_fusion.1
  271.7 5.6 %all_gather.10 = f32[8,8,32,3]{2,1,0,3:T(8,128)S(1)} all-gather(f32[2,8,32,3]{2,1,0,3:T(8,128)S(1)} %pad_maximum_fusion.2), channel_id=1, replica_groups=mesh['groups'=2,'dp'=4,'tensor'=4] {'dp'}, dimensions={0}, use_global_device_ids=true | all-gather | bytes 30720 | tf_op jit(solution)/shard_map/all_gather | solution.py:399
  277.5 0.5 convolution_convert_fusion.5
  278.0 1.0 copy.105
  279.4 0.3 fusion.12
  279.8 0.1 stack.24
  279.9 0.4 fusion.13
  280.4 0.1 stack.25
  280.6 0.3 fusion.14
  281.0 0.1 stack.26
  281.1 9.2 %all_gather.11 = bf16[8,3,32,512]{3,2,0,1:T(8,128)(2,1)} all-gather(bf16[2,3,32,512]{3,2,0,1:T(8,128)(2,1)S(1)} %pad_maximum_fusion), channel_id=1, replica_groups=mesh['groups'=2,'dp'=4,'tensor'=4] {'dp'}, dimensions={0}, use_global_device_ids=true | all-gather | bytes 983040 | tf_op jit(solution)/shard_map/all_gather | solution.py:415
  290.3 2.3 reshape.381
  292.7 0.3 fusion.20
  293.0 0.7 reshape.382
  293.7 1.0 fusion.32
  294.8 0.7 copy.103
  295.6 1.6 fusion.18
  297.2 0.7 convert_element_type.155
  297.9 0.7 convert_element_type.149
  (47 shorter events, 1.3 us)
Async XLA Ops:
  0.6 164.2 %copy-start.6 = (f32[4096]{0:T(1024)S(1)}, f32[4096]{0:T(1024)}, u32[]{:S(2)}) copy-start(f32[4096]{0:T(1024)} %param.14) | copy-start | bytes 49156
  161.6 3.5 %copy-start = (bf16[512,4096]{1,0:T(8,128)(2,1)S(1)}, bf16[512,4096]{1,0:T(8,128)(2,1)}, u32[]{:S(2)}) copy-start(bf16[512,4096]{1,0:T(8,128)(2,1)} %get-tuple-element.5) | copy-start | bytes 12582916
  176.0 3.2 %copy-start.8 = (s32[8]{0:T(128)S(1)}, s32[8]{0:T(128)}, u32[]{:S(2)}) copy-start(s32[8]{0:T(128)} %param.25) | copy-start | bytes 100
  179.4 7.2 %copy-start.1 = (bf16[512,4096]{1,0:T(8,128)(2,1)S(1)}, bf16[512,4096]{1,0:T(8,128)(2,1)}, u32[]{:S(2)}) copy-start(bf16[512,4096]{1,0:T(8,128)(2,1)} %get-tuple-element.5) | copy-start | bytes 12582916
  179.4 7.2 %copy-start.4 = (bf16[4096,512]{1,0:T(8,128)(2,1)S(1)}, bf16[4096,512]{1,0:T(8,128)(2,1)}, u32[]{:S(2)}) copy-start(bf16[4096,512]{1,0:T(8,128)(2,1)} %param.17) | copy-start | bytes 12582916
  235.3 17.3 %copy-start.5 = (bf16[4096,512]{1,0:T(8,128)(2,1)S(1)}, bf16[4096,512]{1,0:T(8,128)(2,1)}, u32[]{:S(2)}) copy-start(bf16[4096,512]{1,0:T(8,128)(2,1)} %param.21) | copy-start | bytes 12582916
  235.3 17.3 %copy-start.7 = (f32[4096]{0:T(1024)S(1)}, f32[4096]{0:T(1024)}, u32[]{:S(2)}) copy-start(f32[4096]{0:T(1024)} %param.19) | copy-start | bytes 49156
  249.4 3.2 %copy-start.10 = (f32[512,4096]{1,0:T(8,128)}, f32[512,4096]{1,0:T(8,128)S(1)}, u32[]{:S(2)}) copy-start(f32[512,4096]{1,0:T(8,128)S(1)} %get-tuple-element.26) | copy-start | bytes 25165828
  256.1 8.1 %copy-start.9 = (s32[8,1]{0,1:T(1,128)S(1)}, s32[8,1]{0,1:T(1,128)}, u32[]{:S(2)}) copy-start(s32[8,1]{0,1:T(1,128)} %param.24) | copy-start | bytes 100
  256.1 8.3 %copy-start.2 = (bf16[1,32,512]{2,1,0:T(8,128)(2,1)S(1)}, bf16[1,32,512]{2,1,0:T(8,128)(2,1)}, u32[]{:S(2)}) copy-start(bf16[1,32,512]{2,1,0:T(8,128)(2,1)} %param.23) | copy-start | bytes 98308
  256.2 8.3 %copy-start.3 = (bf16[1,32,512]{2,1,0:T(8,128)(2,1)S(1)}, bf16[1,32,512]{2,1,0:T(8,128)(2,1)}, u32[]{:S(2)}) copy-start(bf16[1,32,512]{2,1,0:T(8,128)(2,1)} %param.22) | copy-start | bytes 98308

commit v3 on v2

--- a/solution.py
+++ b/solution.py
@@ -49,8 +49,9 @@
 
 
 class Chain:
-    def __init__(self, count, place, own, block, send_sem, recv_sem):
-        self.count, self.place, self.own, self.block = count, place, own, block
+    def __init__(self, count, place, parts, own, block, send_sem, recv_sem):
+        self.count, self.place, self.parts = count, place, parts
+        self.own, self.block = own, block
         self.send_sem, self.recv_sem = send_sem, recv_sem
 
     def arriving(self, step, way):
@@ -61,33 +62,37 @@
         target = self.place + 1 if way == 0 else self.place - 1
         return target, (target < self.count if way == 0 else target >= 0)
 
-    def copy(self, step, way, index, src=None):
-        block = self.block(index)
-        target, _ = self.onward(way)
+    def copy(self, step, way, index, part, first=False):
+        block = self.block(index, part)
         slot = 2 * step + way
         return remote(
-            block if src is None else src,
+            self.own(part) if first else block,
             block,
-            self.send_sem.at[slot],
-            self.recv_sem.at[slot],
-            {"tensor": target},
+            self.send_sem.at[slot, part],
+            self.recv_sem.at[slot, part],
+            {"tensor": self.onward(way)[0]},
         )
 
     def begin(self):
+        for part in range(self.parts):
+            for way in range(2):
+
+                @pl.when(self.onward(way)[1])
+                def _(way=way, part=part):
+                    self.copy(0, way, self.place, part, True).start()
+
+    def receive(self, step, part):
         for way in range(2):
-
-            @pl.when(self.onward(way)[1])
-            def _(way=way):
-                self.copy(0, way, self.place, self.own).start()
-
-    def receive(self, step, way):
-        index, _ = self.arriving(step, way)
-        self.copy(step, way, index).wait_recv()
-        if step + 1 < self.count - 1:
-
-            @pl.when(self.onward(way)[1])
-            def _():
-                self.copy(step + 1, way, index).start()
+            index, there = self.arriving(step, way)
+
+            @pl.when(there)
+            def _(way=way, index=index):
+                self.copy(step, way, index, part).wait_recv()
+                if step + 1 < self.count - 1:
+
+                    @pl.when(self.onward(way)[1])
+                    def _():
+                        self.copy(step + 1, way, index, part).start()
 
     def finish(self):
         for step in range(self.count - 1):
@@ -97,7 +102,23 @@
 
                 @pl.when(there & self.onward(way)[1])
                 def _(step=step, way=way, index=index):
-                    self.copy(step, way, index, self.own if step == 0 else None).wait_send()
+                    for part in range(self.parts):
+                        self.copy(step, way, index, part, step == 0).wait_send()
+
+
+PARTS = 2
+
+
+def parted(ref, parts, part):
+    rows = ref.shape[0] // parts
+    return ref.at[pl.ds(part * rows, rows)]
+
+
+def part_columns(ref, index, width, parts, part):
+    rows = ref.shape[0] // parts
+    return ref.at[
+        pl.ds(part * rows, rows), pl.ds(pl.multiple_of(index * width, width), width)
+    ]
 
 
 def columns(ref, index, width):
@@ -115,21 +136,23 @@
     keep.start()
     greet(*line_targets(count, place))
     chain = Chain(
-        count, place, x_ref, lambda index: columns(out_ref, index, width), send_sem, recv_sem
+        count,
+        place,
+        PARTS,
+        lambda part: parted(x_ref, PARTS, part),
+        lambda index, part: part_columns(out_ref, index, width, PARTS, part),
+        send_sem,
+        recv_sem,
     )
     chain.begin()
     for step in range(count - 1):
-        for way in range(2):
-
-            @pl.when(chain.arriving(step, way)[1])
-            def _(step=step, way=way):
-                chain.receive(step, way)
-
+        for part in range(PARTS):
+            chain.receive(step, part)
     chain.finish()
     keep.wait()
 
 
-def line_gather(x, count):
+def line_gather(x, count, collective_id):
     slots = 2 * (count - 1)
     return pl.pallas_call(
         functools.partial(line_kernel, count),
@@ -138,24 +161,25 @@
         out_specs=pl.BlockSpec(memory_space=pl.ANY),
         scratch_shapes=[
             pltpu.SemaphoreType.DMA,
-            pltpu.SemaphoreType.DMA((slots,)),
-            pltpu.SemaphoreType.DMA((slots,)),
+            pltpu.SemaphoreType.DMA((slots, PARTS)),
+            pltpu.SemaphoreType.DMA((slots, PARTS)),
         ],
-        compiler_params=pltpu.CompilerParams(collective_id=1, has_side_effects=True),
+        compiler_params=pltpu.CompilerParams(collective_id=collective_id, has_side_effects=True),
     )(x)
 
 
-def spread_kernel(
+def plane_kernel(
     sizes,
     tok_ref,
     w_ref,
+    got_ref,
     tok_out,
     w_out,
+    staged,
+    held,
     local_sem,
     tok_send,
     tok_recv,
-    w_send,
-    w_recv,
     g_send,
     g_recv,
     y_send,
@@ -169,10 +193,15 @@
     width = tok_ref.shape[1]
     keeps = (
         pltpu.make_async_copy(tok_ref, columns(tok_out, place, width), local_sem.at[0]),
-        pltpu.make_async_copy(w_ref, w_out.at[place], local_sem.at[1]),
-    )
-    for keep in keeps:
-        keep.start()
+        pltpu.make_async_copy(staged, w_out.at[place], local_sem.at[1]),
+    )
+    loads = (
+        pltpu.make_async_copy(w_ref, staged, local_sem.at[2]),
+        pltpu.make_async_copy(got_ref, held, local_sem.at[3]),
+    )
+    keeps[0].start()
+    for load in loads:
+        load.start()
     other_groups = [lax.rem(group + hop, groups) for hop in range(groups)]
     other_rows = [lax.rem(row + hop, rows) for hop in range(rows)]
     sibling = {"dp": row * 2 + 1 - core}
@@ -185,118 +214,140 @@
         return (group_at * rows + row_at) * 2 + core_at
 
     mine = at(group, row, core)
-    weights = Chain(
-        count, place, w_ref.at[mine], lambda index: w_out.at[index, mine], w_send, w_recv
-    )
+    others = [lax.rem(place + 1 + slot, count) for slot in range(count - 1)]
+    stores = [
+        pltpu.make_async_copy(held.at[index], w_out.at[index, mine], local_sem.at[4 + slot])
+        for slot, index in enumerate(others)
+    ]
     toks = Chain(
-        count, place, tok_ref, lambda index: columns(tok_out, index, width), tok_send, tok_recv
-    )
-
-    def across(step, way, hop, outward):
-        index, slot = weights.arriving(step, way)[0], 2 * step + way
-        sems = g_send.at[slot, hop - 1], g_recv.at[slot, hop - 1]
-        there = w_out.at[index, mine]
-        source = at(other_groups[groups - hop], row, core)
-        here = w_out.at[index, source]
+        count,
+        place,
+        PARTS,
+        lambda part: parted(tok_ref, PARTS, part),
+        lambda index, part: part_columns(tok_out, index, width, PARTS, part),
+        tok_send,
+        tok_recv,
+    )
+
+    def across(slot, hop, hop_row, outward):
+        index = others[slot]
+        sems = g_send.at[slot, hop - 1, hop_row], g_recv.at[slot, hop - 1, hop_row]
+        block_row = other_rows[(rows - hop_row) % rows]
+        there = w_out.at[index, at(group, block_row, core)]
+        here = w_out.at[index, at(other_groups[groups - hop], block_row, core)]
         target = {"groups": other_groups[hop]}
-        block = there if outward else here
-        return remote(block, block, *sems, target)
-
-    def along(step, way, hop_g, hop, outward):
-        index, slot = weights.arriving(step, way)[0], 2 * step + way
+        source = got_ref.at[index] if hop_row == 0 else there
+        return remote(source, there if outward else here, *sems, target)
+
+    def along(slot, hop_g, hop, outward):
+        index = others[slot]
         sems = y_send.at[slot, hop_g, hop - 1], y_recv.at[slot, hop_g, hop - 1]
         block_group = other_groups[(groups - hop_g) % groups]
         there = w_out.at[index, at(block_group, row, core)]
         here = w_out.at[index, at(block_group, other_rows[rows - hop], core)]
         target = {"dp": other_rows[hop] * 2 + core}
         block = there if outward else here
+        if hop_g == 0:
+            return remote(got_ref.at[index], block, *sems, target)
         return remote(block, block, *sems, target)
 
-    def beside(step, way, hop_g, hop, outward):
-        index, slot = weights.arriving(step, way)[0], 2 * step + way
+    def beside(slot, hop_g, hop, outward):
+        index = others[slot]
         sems = c_send.at[slot, hop_g, hop], c_recv.at[slot, hop_g, hop]
         block_group = other_groups[(groups - hop_g) % groups]
         block_row = other_rows[(rows - hop) % rows]
         there = w_out.at[index, at(block_group, block_row, core)]
         here = w_out.at[index, at(block_group, block_row, 1 - core)]
         block = there if outward else here
+        if hop_g == 0 and hop == 0:
+            return remote(got_ref.at[index], block, *sems, sibling)
         return remote(block, block, *sems, sibling)
 
-    def first(step, way):
-        weights.receive(step, way)
+    def rows_last(slot):
+        return slot % 2 == 0
+
+    def first(slot):
         for hop in range(1, groups):
-            across(step, way, hop, True).start()
+            across(slot, hop, 0, True).start()
         for hop in range(1, rows):
-            along(step, way, 0, hop, True).start()
-        beside(step, way, 0, 0, True).start()
-
-    def second(step, way):
+            along(slot, 0, hop, True).start()
+        beside(slot, 0, 0, True).start()
+
+    def second(slot):
         for hop_g in range(1, groups):
-            across(step, way, hop_g, False).wait_recv()
+            across(slot, hop_g, 0, False).wait_recv()
+            if rows_last(slot):
+                for hop in range(1, rows):
+                    along(slot, hop_g, hop, True).start()
+            beside(slot, hop_g, 0, True).start()
+        for hop in range(1, rows):
+            along(slot, 0, hop, False).wait_recv()
+            if not rows_last(slot):
+                for hop_g in range(1, groups):
+                    across(slot, hop_g, hop, True).start()
+            beside(slot, 0, hop, True).start()
+
+    def third(slot):
+        for hop_g in range(1, groups):
             for hop in range(1, rows):
-                along(step, way, hop_g, hop, True).start()
-            beside(step, way, hop_g, 0, True).start()
-
-    def third(step, way):
-        for hop_g in range(groups):
-            for hop in range(1, rows):
-                along(step, way, hop_g, hop, False).wait_recv()
-                beside(step, way, hop_g, hop, True).start()
-
-    def last(step, way):
+                if rows_last(slot):
+                    along(slot, hop_g, hop, False).wait_recv()
+                else:
+                    across(slot, hop_g, hop, False).wait_recv()
+                beside(slot, hop_g, hop, True).start()
+
+    def last(slot):
         for hop_g in range(groups):
             for hop in range(rows):
-                beside(step, way, hop_g, hop, False).wait_recv()
-        for hop in range(1, groups):
-            across(step, way, hop, True).wait_send()
-        for hop_g in range(groups):
-            for hop in range(1, rows):
-                along(step, way, hop_g, hop, True).wait_send()
-            for hop in range(rows):
-                beside(step, way, hop_g, hop, True).wait_send()
-
-    def each_way(step, act):
-        for way in range(2):
-
-            @pl.when(weights.arriving(step, way)[1])
-            def _(way=way):
-                act(step, way)
-
-    weights.begin()
+                beside(slot, hop_g, hop, False).wait_recv()
+                beside(slot, hop_g, hop, True).wait_send()
+                if hop_g and (hop == 0 or not rows_last(slot)):
+                    across(slot, hop_g, hop, True).wait_send()
+                if hop and (hop_g == 0 or rows_last(slot)):
+                    along(slot, hop_g, hop, True).wait_send()
+
     toks.begin()
+    for slot in range(count - 1):
+        first(slot)
+    for load in loads:
+        load.wait()
+    keeps[1].start()
+    for store in stores:
+        store.start()
     for step in range(count - 1):
-        each_way(step, first)
+        for part in range(PARTS):
+            toks.receive(step, part)
+        second(step)
         if step >= 1:
-            each_way(step - 1, second)
-        each_way(step, toks.receive)
-        if step >= 1:
-            each_way(step - 1, third)
-    each_way(count - 2, second)
-    each_way(count - 2, third)
-    for step in range(count - 1):
-        each_way(step, last)
-    weights.finish()
+            third(step - 1)
+    third(count - 2)
+    for slot in range(count - 1):
+        last(slot)
     toks.finish()
-    for keep in keeps:
-        keep.wait()
-
-
-def spread(tokens, w_slices, groups, rows, count):
-    slots = 2 * (count - 1)
-    sems = [(slots,), (slots,), (slots, groups - 1), (slots, groups, rows - 1)]
+    for copy in (*keeps, *stores):
+        copy.wait()
+
+
+def plane(context, w_slices, gathered, groups, rows, count):
+    slots = count - 1
+    sems = [(2 * slots, PARTS), (slots, groups - 1, rows), (slots, groups, rows - 1)]
     sems.append((slots, groups, rows))
     return pl.pallas_call(
-        functools.partial(spread_kernel, (groups, rows, count)),
+        functools.partial(plane_kernel, (groups, rows, count)),
         out_shape=(
-            jax.ShapeDtypeStruct((tokens.shape[0], tokens.shape[1] * count), tokens.dtype),
+            jax.ShapeDtypeStruct(
+                (context.shape[0], context.shape[1] * count), context.dtype
+            ),
             jax.ShapeDtypeStruct((count,) + w_slices.shape, w_slices.dtype),
         ),
-        in_specs=[pl.BlockSpec(memory_space=pl.ANY)] * 2,
+        in_specs=[pl.BlockSpec(memory_space=pl.ANY)] * 3,
         out_specs=(pl.BlockSpec(memory_space=pl.ANY),) * 2,
-        scratch_shapes=[pltpu.SemaphoreType.DMA((2,))]
+        scratch_shapes=[pltpu.VMEM(w_slices.shape, w_slices.dtype), pltpu.VMEM(gathered.shape, w_slices.dtype), pltpu.SemaphoreType.DMA((3 + count,))]
         + [pltpu.SemaphoreType.DMA(shape) for shape in sems for _ in range(2)],
-        compiler_params=pltpu.CompilerParams(collective_id=0, has_side_effects=True),
-    )(tokens, w_slices)
+        compiler_params=pltpu.CompilerParams(
+            collective_id=1, has_side_effects=True, vmem_limit_bytes=16 << 20
+        ),
+    )(context, w_slices, gathered)
 
 
 def shards(
@@ -324,15 +375,14 @@
     groups, dp_count = lax.axis_size("groups"), lax.axis_size("dp")
     tensor_count = lax.axis_size("tensor")
     asked = lax.all_gather(jnp.stack([dec_query, grad_out]), "dp", axis=1, tiled=True)
-    gathered_in, out_full = spread(
-        tokens.reshape(row_count, part_width),
-        w_out.reshape(groups * dp_count, local_cols // (groups * dp_count), w_out.shape[1]),
-        groups,
-        dp_count // 2,
-        tensor_count,
-    )
+    slices = groups * dp_count
+    slice_rows = local_cols // slices
+    slice_at = lax.axis_index("groups") * dp_count + lax.axis_index("dp")
+    out_slice = lax.dynamic_slice_in_dim(w_out, slice_at * slice_rows, slice_rows, 0)
+    gathered_in = line_gather(tokens.reshape(row_count, part_width), tensor_count, 0)
+    out_slice, gathered_in = lax.optimization_barrier((out_slice, gathered_in))
+    out_slice = lax.all_gather(out_slice, "tensor", axis=0, tiled=False)
     full_width = gathered_in.shape[1]
-    out_full = out_full.reshape(tensor_count * local_cols, full_width)
     inputs_f = gathered_in.reshape(row_count, full_width).astype(jnp.float32)
     normed = norm_rows(inputs_f, ln_gain).astype(jnp.bfloat16)
 
@@ -363,7 +413,15 @@
         .astype(jnp.bfloat16)
         .reshape(row_count, local_cols)
     )
-    all_context = line_gather(context, tensor_count)
+    all_context, out_full = plane(
+        context,
+        w_out.reshape(slices, slice_rows, full_width),
+        out_slice,
+        groups,
+        dp_count // 2,
+        tensor_count,
+    )
+    out_full = out_full.reshape(tensor_count * local_cols, full_width)
     summed = jnp.dot(all_context, out_full, preferred_element_type=jnp.float32)
     encoded = norm_rows(inputs_f + summed, final_gain).astype(jnp.bfloat16)
     cross_keys = jnp.dot(encoded, w_cross_key, preferred_element_type=jnp.float32).astype(

time: 299 us -> 257 us (0.86)
  Pallas kernels: 202 us -> 136 us
  waiting for transfers between devices: 0 us -> 17.8 us
  between operations: 1.05 us -> 14.5 us
  other arithmetic: 14.6 us -> 8.26 us
  matrix products: 43.7 us -> 40.6 us
    pallas_call x1, Pallas kernels: 161 us -> 62.7 us  [plane(): pl.pallas_call(functools.partial(plane_kernel, (groups, rows, count)), ou...]
    pallas_call x1, Pallas kernels: 40.9 us -> 73.1 us  [line_gather(): pl.pallas_call(functools.partial(line_kernel, count), out_shape=jax.Shape...]
    all_gather x0 -> x1, waiting for transfers between devices: none -> 17.8 us  [shards(): out_slice = lax.all_gather(out_slice, 'tensor', axis=0, tiled=False)]
    sub x1, other arithmetic: 7.21 us -> 1.74 us  [shards(): scores - row_peak]
    dot_general x1, matrix products: 2.37 us -> 6.95 us  [shards(): jnp.dot(encoded, w_cross_value, preferred_element_type=jnp.float32)]
  transfers between devices with their start and end apart: 0 -> 1, of which waited for: 0 -> 1; matrix products, arithmetic and copies ran while one was open for 0% -> 9% of each run, Pallas kernels for 0% -> 0%
where the time goes in v3:
time: 257 us; the launch traced here: 256 us
  Pallas kernels  136 us (53%)
  matrix products  40.6 us (16%)
  blocking collectives  20.7 us (8%)
  local copies, waits for them, and re-layouts  18.9 us (7%)
  waiting for transfers between devices  17.8 us (7%)
  between operations  14.5 us (6%)
  other arithmetic  8.26 us (3%)
    pallas_call x1, Pallas kernels, line_gather(): pl.pallas_call(functools.partial(line_kernel, count), out_shape=jax.Shape...  73.1 us
    pallas_call x1, Pallas kernels, plane(): pl.pallas_call(functools.partial(plane_kernel, (groups, rows, count)), ou...  62.7 us
    all_gather x1, waiting for transfers between devices, shards(): out_slice = lax.all_gather(out_slice, 'tensor', axis=0, tiled=False)  17.8 us
    dot_general x1, matrix products, shards(): summed = jnp.dot(all_context, out_full, preferred_element_type=jnp.float32)  13 us
    dot_general x3, matrix products, project(): jnp.dot(normed, weight, preferred_element_type=jnp.float32)  10.3 us
    all_gather x1, blocking collectives, shards(): all_partials = lax.all_gather(partials, 'dp', axis=0, tiled=True)  9.17 us
    dot_general x1, matrix products, shards(): jnp.dot(encoded, w_cross_value, preferred_element_type=jnp.float32)  6.95 us
    dot_general x1, matrix products, shards(): jnp.dot(encoded, w_cross_key, preferred_element_type=jnp.float32)  6.94 us
  transfers between devices with their start and end apart: 1, of which 1 were waited for; matrix products, arithmetic and copies ran while one was open for 9% of the time, Pallas kernels for 0%

profile of v3, /device:TPU:0, one launch (start us, length us, event | category | flops | bytes accessed | tf_op | source)
XLA Modules:
  0.0 256.5 jit_solution(1414494218759246690)
XLA Ops:
  7.2 73.1 %shard_map.148 = bf16[512,4096]{1,0:T(8,128)(2,1)} custom-call(bf16[512,1024]{1,0:T(8,128)(2,1)} %bitcast.113), custom_call_target="tpu_custom_call" | custom-call | tf_op jit(solution)/shard_map/pallas_call | solution.py:157
  80.3 1.9 constant_dynamic-slice_fusion
  82.2 3.2 %fusion.1 = f32[512]{0:T(512)S(1)} fusion(bf16[512,4096]{1,0:T(8,128)(2,1)} %shard_map.148), kind=kLoop, calls=%fused_computation.4 | loop fusion | flops 6290944 | bytes 4196352 | tf_op jit(solution)/shard_map/reduce_sum | solution.py:17
  85.5 0.2 copy-done.2
  85.6 4.7 %convolution_convert_fusion.3 = bf16[512,512]{1,0:T(8,128)(2,1)S(1)} fusion(bf16[4096,512]{1,0:T(8,128)(2,1)} %param.15, bf16[512,4096]{1,0:T(8,128)(2,1)S(1)} %copy-done.2, f32[4096]{0:T(1024)S(1)} %copy-done.7, f32[512]{0:T(512)S(1)} %add_rsqrt_fusion.1), kind=kOutput, calls=%fused_computation.20 | convolution fusion | flops 2156134400 | bytes 8931328 | tf_op jit(solution)/shard_map/dot_general | solution.py:391
  90.4 2.4 convolution_convert_fusion.2
  92.8 3.2 %convolution_convert_fusion.4 = bf16[512,512]{1,0:T(8,128)(2,1)} fusion(bf16[4096,512]{1,0:T(8,128)(2,1)S(1)} %copy-done.6, bf16[512,4096]{1,0:T(8,128)(2,1)S(1)} %copy-done.2, f32[4096]{0:T(1024)S(1)} %copy-done.7, f32[512]{0:T(512)S(1)} %add_rsqrt_fusion.1), kind=kOutput, calls=%fused_computation.21 | convolution fusion | flops 2156134400 | bytes 8931328 | tf_op jit(solution)/shard_map/dot_general | solution.py:391
  96.0 0.5 reshape.386
  96.5 0.5 reshape.387
  97.0 1.6 reshape.385
  98.9 0.7 fusion.21
  99.6 1.7 fusion.57
  101.3 0.5 fusion.10
  101.9 0.6 copy.113
  102.5 0.6 reshape.388.tok_ref
  103.1 0.7 reshape.382
  103.9 6.0 %all_gather.15 = bf16[2,4,32,512]{3,2,1,0:T(8,128)(2,1)S(1)} all-gather(bf16[2,1,32,512]{3,2,1,0:T(8,128)(2,1)S(1)} %pad_maximum_fusion.1), channel_id=1, replica_groups=mesh['groups'=2,'dp'=4,'tensor'=4] {'dp'}, dimensions={1}, use_global_device_ids=true | all-gather | bytes 327680 | tf_op jit(solution)/shard_map/all_gather | solution.py:377
  110.0 0.1 select_reduce_fusion
  110.6 17.8 %all-gather.3.cloned.1.call-done = bf16[256,4096]{1,0:T(8,128)(2,1)} async-done(((bf16[64,4096]{1,0:T(8,128)(2,1)}), bf16[256,4096]{1,0:T(8,128)(2,1)}) %all-gather.3.cloned.1.call-update) | async-done | bytes 2097168 | tf_op jit(solution)/shard_map/all_gather | solution.py:384
  128.4 2.2 copy-done
  130.6 1.6 copy-done.1
  132.1 62.7 %shard_map.149 = (bf16[512,2048]{1,0:T(8,128)(2,1)S(1)}, bf16[4,8,64,4096]{3,2,1,0:T(8,128)(2,1)S(1)}) custom-call(bf16[512,512]{1,0:T(8,128)(2,1)S(1)} %reshape.388.tok_ref, bf16[8,64,4096]{2,1,0:T(8,128)(2,1)S(1)} %bitcast.109, bf16[4,64,4096]{2,1,0:T(8,128)(2,1)S(1)} %bitcast.110), custom_call_target="tpu_custom_call" | custom-call | tf_op jit(solution)/shard_map/pallas_call | solution.py:335
  194.8 13.0 %multiply_reduce_fusion = (f32[512]{0:T(512)S(1)}, f32[512,4096]{1,0:T(8,128)}) fusion(bf16[512,2048]{1,0:T(8,128)(2,1)S(1)} %get-tuple-element.9, bf16[2048,4096]{1,0:T(8,128)(2,1)S(1)} %bitcast.111, bf16[512,4096]{1,0:T(8,128)(2,1)} %shard_map.148), kind=kOutput, calls=%fused_computation.8 | convolution fusion | flops 8598323200 | bytes 31459328 | tf_op jit(solution)/shard_map/dot_general | solution.py:425
  207.8 6.9 %convolution_convert_fusion = bf16[512,512]{1,0:T(8,128)(2,1)S(1)} fusion(bf16[4096,512]{1,0:T(8,128)(2,1)} %param.21, f32[512,4096]{1,0:T(8,128)} %get-tuple-element.30, f32[4096]{0:T(1024)S(1)} %copy-done.8, f32[512]{0:T(512)S(1)} %add_rsqrt_fusion), kind=kOutput, calls=%fused_computation.17 | convolution fusion | flops 2154037248 | bytes 13125632 | tf_op jit(solution)/shard_map/dot_general | solution.py:430
  214.8 0.5 reshape.390
  215.3 0.6 copy.94
  215.9 6.9 %convolution_convert_fusion.1 = bf16[512,512]{1,0:T(8,128)(2,1)S(1)} fusion(bf16[4096,512]{1,0:T(8,128)(2,1)} %param.20, f32[512,4096]{1,0:T(8,128)} %get-tuple-element.30, f32[4096]{0:T(1024)S(1)} %copy-done.8, f32[512]{0:T(512)S(1)} %add_rsqrt_fusion), kind=kOutput, calls=%fused_computation.18 | convolution fusion | flops 2154037248 | bytes 13125632 | tf_op jit(solution)/shard_map/dot_general | solution.py:427
  222.9 0.5 reshape.389
  223.4 0.6 copy.91
  224.0 0.3 fusion.58
  224.3 0.3 fusion.26
  224.6 0.3 fusion.14
  224.9 0.3 fusion.12
  225.3 0.3 multiply_reduce_fusion.1
  225.6 5.6 %all_gather.18 = f32[8,8,32,3]{2,1,0,3:T(8,128)S(1)} all-gather(f32[2,8,32,3]{2,1,0,3:T(8,128)S(1)} %pad_maximum_fusion.2), channel_id=1, replica_groups=mesh['groups'=2,'dp'=4,'tensor'=4] {'dp'}, dimensions={0}, use_global_device_ids=true | all-gather | bytes 30720 | tf_op jit(solution)/shard_map/all_gather | solution.py:457
  231.4 0.5 convolution_convert_fusion.5
  231.9 1.0 copy.105
  233.4 0.1 stack.24
  233.5 0.4 fusion.13
  234.0 0.1 stack.25
  234.2 0.1 stack.26
  234.4 9.2 %all_gather.19 = bf16[8,3,32,512]{3,2,0,1:T(8,128)(2,1)} all-gather(bf16[2,3,32,512]{3,2,0,1:T(8,128)(2,1)S(1)} %pad_maximum_fusion), channel_id=1, replica_groups=mesh['groups'=2,'dp'=4,'tensor'=4] {'dp'}, dimensions={0}, use_global_device_ids=true | all-gather | bytes 983040 | tf_op jit(solution)/shard_map/all_gather | solution.py:473
  243.5 2.3 reshape.381
  245.9 0.3 fusion.20
  246.2 0.7 convert_element_type.149
  247.0 1.0 fusion.32
  248.2 0.7 fusion.18
  248.9 0.7 convert_element_type.155
  (51 shorter events, 1.8 us)
Async XLA Ops:
  7.2 121.2 %all-gather.3.cloned.1.call-start = ((), (), s32[]{:S(2)}) async-start(), calls=%async_computation | async-start | bytes 2621440 | tf_op jit(solution)/shard_map/all_gather | solution.py:384
  80.3 5.2 %copy-start.7 = (f32[4096]{0:T(1024)S(1)}, f32[4096]{0:T(1024)}, u32[]{:S(2)}) copy-start(f32[4096]{0:T(1024)} %param.14) | copy-start | bytes 49156
  82.2 3.5 %copy-start.2 = (bf16[512,4096]{1,0:T(8,128)(2,1)S(1)}, bf16[512,4096]{1,0:T(8,128)(2,1)}, u32[]{:S(2)}) copy-start(bf16[512,4096]{1,0:T(8,128)(2,1)} %shard_map.148) | copy-start | bytes 12582916
  85.6 4.7 %copy-start.5 = (bf16[4096,512]{1,0:T(8,128)(2,1)S(1)}, bf16[4096,512]{1,0:T(8,128)(2,1)}, u32[]{:S(2)}) copy-start(bf16[4096,512]{1,0:T(8,128)(2,1)} %param.16) | copy-start | bytes 12582916
  90.4 2.4 copy-start.6
  96.0 2.7 %copy-start.9 = (s32[8]{0:T(128)S(1)}, s32[8]{0:T(128)}, u32[]{:S(2)}) copy-start(s32[8]{0:T(128)} %param.25) | copy-start | bytes 100
  101.3 1.8 copy-start.3
  101.3 2.5 copy-start.4
  101.9 8.0 %copy-start.10 = (s32[8,1]{0,1:T(1,128)S(1)}, s32[8,1]{0,1:T(1,128)}, u32[]{:S(2)}) copy-start(s32[8,1]{0,1:T(1,128)} %param.24) | copy-start | bytes 100
  128.4 2.2 copy-start
  130.6 1.6 copy-start.1
  194.8 13.0 %copy-start.8 = (f32[4096]{0:T(1024)S(1)}, f32[4096]{0:T(1024)}, u32[]{:S(2)}) copy-start(f32[4096]{0:T(1024)} %param.19) | copy-start | bytes 49156
Sparse Core Ops, SparseCore 0:
  82.3 46.0 all-gather.2
